TPU v7x, 512 devices: a whole 4x8x8 slice. The times are simulated.
512 devices in a mesh: wide: 64 (over z, y), narrow: 8 (over x, core).
Axes of the slice: x: 4, y: 8, z: 8, core: 2. Of those that a mesh axis runs over, the one named last changes fastest.
Arguments:
- snapshots: float32 [128, 524288], P('wide', 'narrow'), may hold values from -1000 to 1000
Outputs:
- q_scaled: float32 [524288, 128], P(('narrow', 'wide'))
- r_scaled: float32 [128, 128], replicated
All inputs are finite; a program needn't handle non-finite values.
Results may differ from a plain program's by a relative error of at most 0.0003.
Values sent between devices are 32-bit elements; how exact they have to be, the bound alone decides.
No kernel may reach another device: no remote copies, remote signals or barrier semaphores. Data moves between devices by JAX's collectives and lax.ppermute only.
A program may use at most 64 MiB of HBM per device.

v0:
```python
import math

import jax
import jax.numpy as jnp
from jax import lax
from jax.sharding import PartitionSpec as P


def shifted(block, axis, distance):
    devices = range(lax.axis_size(axis))
    route = [(i - distance, i) for i in devices if i - distance in devices]
    return lax.ppermute(block, axis, route)


def inner(left, right):
    return lax.dot_general(
        left,
        right,
        (((1,), (1,)), ((), ())),
        precision=lax.Precision.HIGHEST,
        preferred_element_type=jnp.float32,
    )


def product(left, right):
    return jnp.dot(left, right, precision=lax.Precision.HIGHEST, preferred_element_type=jnp.float32)


def cholesky_pass(columns, gram_matrix):
    lower_factor = jnp.linalg.cholesky(gram_matrix)
    solved = jax.scipy.linalg.solve_triangular(lower_factor, columns, lower=True)
    return (solved, jnp.transpose(lower_factor))


def factor_twice(columns):
    first_rows, first_upper = cholesky_pass(columns, inner(columns, columns))
    second_rows, second_upper = cholesky_pass(first_rows, inner(first_rows, first_rows))
    return (second_rows, product(second_upper, first_upper))


def stack_pair(first_upper, second_upper):
    return jnp.concatenate([jnp.transpose(first_upper), jnp.transpose(second_upper)], axis=1)


def axis_digit(axis_name, bit_number):
    if axis_name == "wide":
        position = lax.axis_index("wide")
    else:
        position = lax.axis_index("narrow")
    return position // (1 << bit_number) % 2


def level_list():
    wide_levels = [
        ("wide", bit_number) for bit_number in range(lax.axis_size("wide").bit_length() - 1)
    ]
    narrow_levels = [
        ("narrow", bit_number) for bit_number in range(lax.axis_size("narrow").bit_length() - 1)
    ]
    return wide_levels + narrow_levels


def pull_up(value, axis_name, bit_number):
    if axis_name == "wide":
        return shifted(value, "wide", -(1 << bit_number))
    return shifted(value, "narrow", -(1 << bit_number))


def push_down(values, axis_name, bit_number):
    if axis_name == "wide":
        return shifted((values[0], values[1]), "wide", 1 << bit_number)
    return shifted((values[0], values[1]), "narrow", 1 << bit_number)


def tree_factor(leaf_rows, leaf_upper, level_order):
    factor_order = leaf_upper.shape[0]
    active = jnp.array(True)
    keepers = []
    partners = []
    factor_list = []
    upper_now = leaf_upper
    for axis_name, bit_number in level_order:
        bit_value = axis_digit(axis_name, bit_number)
        keepers.append(jnp.logical_and(active, bit_value == 0))
        partners.append(jnp.logical_and(active, bit_value == 1))
        received = pull_up(upper_now, axis_name, bit_number)
        factors, upper_now = factor_twice(stack_pair(upper_now, received))
        factor_list.append(factors)
        active = jnp.logical_and(active, bit_value == 0)
    carry_rows = jnp.eye(factor_order, dtype=jnp.float32)
    final_upper = upper_now
    for position in range(len(level_order) - 1, -1, -1):
        axis_name, bit_number = level_order[position]
        factors = factor_list[position]
        own_part = product(carry_rows, factors[:, :factor_order])
        sent_part = product(carry_rows, factors[:, factor_order:])
        got_part, got_upper = push_down((sent_part, final_upper), axis_name, bit_number)
        carry_rows = jnp.where(
            keepers[position], own_part, jnp.where(partners[position], got_part, carry_rows)
        )
        final_upper = jnp.where(partners[position], got_upper, final_upper)
    return (product(carry_rows, leaf_rows), final_upper)


def shards(snapshots):
    block_cols = lax.all_to_all(snapshots, "wide", split_axis=1, concat_axis=0, tiled=True)
    leaf_rows, leaf_upper = factor_twice(block_cols)
    level_order = level_list()
    orth_rows, upper_factor = tree_factor(leaf_rows, leaf_upper, level_order)
    total_rows = block_cols.shape[1] * lax.axis_size("wide") * lax.axis_size("narrow")
    root_rows = math.sqrt(total_rows)
    return (jnp.transpose(orth_rows) * root_rows, upper_factor / root_rows)


def solution(mesh):
    in_specs = (P("wide", "narrow"),)
    out_specs = (P(("narrow", "wide"), None), P())
    return jax.shard_map(shards, mesh=mesh, in_specs=in_specs, out_specs=out_specs, check_vma=False)
```

profile of v0, /device:TPU:64, one launch (start us, length us, event | category | flops | bytes accessed | tf_op | source)
XLA Modules:
  0.0 681.5 jit_solution(5763520571277868517)
XLA Ops:
  0.6 15.8 %all-to-all-start = ((f32[2,64,1024]{2,0,1:T(2,128)}), f32[2,64,1024]{2,0,1:T(2,128)S(1)}, u32[]{:S(2)}, u32[]{:S(2)}) async-start(f32[2,64,1024]{2,0,1:T(2,128)} %bitcast.268), calls=%async_computation | async-start | bytes 1048576 | tf_op jit(solution)/shard_map/all_to_all | solution.py:106
  16.7 18.5 %all-to-all-done = f32[2,64,1024]{2,0,1:T(2,128)S(1)} async-done(((f32[2,64,1024]{2,0,1:T(2,128)}), f32[2,64,1024]{2,0,1:T(2,128)S(1)}, u32[]{:S(2)}, u32[]{:S(2)}) %all-to-all-start) | async-done | bytes 524320 | tf_op jit(solution)/shard_map/all_to_all | solution.py:106
  36.3 11.7 %cholesky.314 = f32[128,128]{1,0:T(8,128)S(1)} custom-call(f32[128,128]{1,0:T(8,128)S(1)} %fusion.96), custom_call_target="Cholesky" | custom-call | tf_op jit(solution)/shard_map/jit(cholesky)/cholesky | solution.py:30
  49.3 9.8 %custom-call.26 = f32[1,128,128]{1,2,0:T(8,128)S(1)} custom-call(f32[1,128,128]{2,1,0:T(8,128)S(1)} %fusion.100), custom_call_target="InvertDiagBlocksLowerTriangular" | custom-call | tf_op jit(solution)/shard_map/jit(_solve_triangular)/triangular_solve | solution.py:31
  60.5 11.7 %cholesky.325 = f32[128,128]{1,0:T(8,128)S(1)} custom-call(f32[128,128]{1,0:T(8,128)S(1)} %fusion.93), custom_call_target="Cholesky" | custom-call | tf_op jit(solution)/shard_map/jit(cholesky)/cholesky | solution.py:30
  75.3 9.8 %custom-call.27 = f32[1,128,128]{1,2,0:T(8,128)S(1)} custom-call(f32[1,128,128]{2,1,0:T(8,128)S(1)} %select_bitcast_fusion.18), custom_call_target="InvertDiagBlocksLowerTriangular" | custom-call | tf_op jit(solution)/shard_map/jit(_solve_triangular)/triangular_solve | solution.py:31
  91.8 11.7 %cholesky.336 = f32[128,128]{1,0:T(8,128)S(1)} custom-call(f32[128,128]{1,0:T(8,128)S(1)} %fusion.90), custom_call_target="Cholesky" | custom-call | tf_op jit(solution)/shard_map/jit(cholesky)/cholesky | solution.py:30
  104.9 9.8 %custom-call.28 = f32[1,128,128]{1,2,0:T(8,128)S(1)} custom-call(f32[1,128,128]{2,1,0:T(8,128)S(1)} %select_bitcast_fusion.17), custom_call_target="InvertDiagBlocksLowerTriangular" | custom-call | tf_op jit(solution)/shard_map/jit(_solve_triangular)/triangular_solve | solution.py:31
  115.4 11.7 %cholesky.347 = f32[128,128]{1,0:T(8,128)S(1)} custom-call(f32[128,128]{1,0:T(8,128)S(1)} %fusion.88), custom_call_target="Cholesky" | custom-call | tf_op jit(solution)/shard_map/jit(cholesky)/cholesky | solution.py:30
  130.0 19.6 %custom-call.45 = f32[1,128,128]{1,2,0:T(8,128)S(1)} custom-call(f32[1,128,128]{2,1,0:T(8,128)S(1)} %select_bitcast_fusion), custom_call_target="InvertDiagBlocksLowerTriangular" | custom-call | tf_op jit(solution)/shard_map/jit(_solve_triangular)/triangular_solve | solution.py:31
  157.2 11.7 %cholesky.358 = f32[128,128]{1,0:T(8,128)S(1)} custom-call(f32[128,128]{1,0:T(8,128)S(1)} %fusion.87), custom_call_target="Cholesky" | custom-call | tf_op jit(solution)/shard_map/jit(cholesky)/cholesky | solution.py:30
  170.2 9.8 %custom-call.29 = f32[1,128,128]{1,2,0:T(8,128)S(1)} custom-call(f32[1,128,128]{2,1,0:T(8,128)S(1)} %select_bitcast_fusion.16), custom_call_target="InvertDiagBlocksLowerTriangular" | custom-call | tf_op jit(solution)/shard_map/jit(_solve_triangular)/triangular_solve | solution.py:31
  180.7 11.7 %cholesky.369 = f32[128,128]{1,0:T(8,128)S(1)} custom-call(f32[128,128]{1,0:T(8,128)S(1)} %fusion.85), custom_call_target="Cholesky" | custom-call | tf_op jit(solution)/shard_map/jit(cholesky)/cholesky | solution.py:30
  195.4 10.2 %custom-call.44 = f32[1,128,128]{1,2,0:T(8,128)S(1)} custom-call(f32[1,128,128]{2,1,0:T(8,128)S(1)} %select_bitcast_fusion.1), custom_call_target="InvertDiagBlocksLowerTriangular" | custom-call | tf_op jit(solution)/shard_map/jit(_solve_triangular)/triangular_solve | solution.py:31
  216.2 11.7 %cholesky.380 = f32[128,128]{1,0:T(8,128)S(1)} custom-call(f32[128,128]{1,0:T(8,128)S(1)} %fusion.84), custom_call_target="Cholesky" | custom-call | tf_op jit(solution)/shard_map/jit(cholesky)/cholesky | solution.py:30
  229.2 9.8 %custom-call.30 = f32[1,128,128]{1,2,0:T(8,128)S(1)} custom-call(f32[1,128,128]{2,1,0:T(8,128)S(1)} %select_bitcast_fusion.15), custom_call_target="InvertDiagBlocksLowerTriangular" | custom-call | tf_op jit(solution)/shard_map/jit(_solve_triangular)/triangular_solve | solution.py:31
  239.8 11.7 %cholesky.391 = f32[128,128]{1,0:T(8,128)S(1)} custom-call(f32[128,128]{1,0:T(8,128)S(1)} %fusion.82), custom_call_target="Cholesky" | custom-call | tf_op jit(solution)/shard_map/jit(cholesky)/cholesky | solution.py:30
  254.4 10.0 %custom-call.43 = f32[1,128,128]{1,2,0:T(8,128)S(1)} custom-call(f32[1,128,128]{2,1,0:T(8,128)S(1)} %select_bitcast_fusion.2), custom_call_target="InvertDiagBlocksLowerTriangular" | custom-call | tf_op jit(solution)/shard_map/jit(_solve_triangular)/triangular_solve | solution.py:31
  271.7 11.7 %cholesky.402 = f32[128,128]{1,0:T(8,128)S(1)} custom-call(f32[128,128]{1,0:T(8,128)S(1)} %fusion.81), custom_call_target="Cholesky" | custom-call | tf_op jit(solution)/shard_map/jit(cholesky)/cholesky | solution.py:30
  284.7 9.8 %custom-call.31 = f32[1,128,128]{1,2,0:T(8,128)S(1)} custom-call(f32[1,128,128]{2,1,0:T(8,128)S(1)} %select_bitcast_fusion.14), custom_call_target="InvertDiagBlocksLowerTriangular" | custom-call | tf_op jit(solution)/shard_map/jit(_solve_triangular)/triangular_solve | solution.py:31
  295.3 11.7 %cholesky.413 = f32[128,128]{1,0:T(8,128)S(1)} custom-call(f32[128,128]{1,0:T(8,128)S(1)} %fusion.79), custom_call_target="Cholesky" | custom-call | tf_op jit(solution)/shard_map/jit(cholesky)/cholesky | solution.py:30
  309.9 10.2 %custom-call.42 = f32[1,128,128]{1,2,0:T(8,128)S(1)} custom-call(f32[1,128,128]{2,1,0:T(8,128)S(1)} %select_bitcast_fusion.3), custom_call_target="InvertDiagBlocksLowerTriangular" | custom-call | tf_op jit(solution)/shard_map/jit(_solve_triangular)/triangular_solve | solution.py:31
  321.7 5.8 collective-permute-done.4
  328.0 11.7 %cholesky.424 = f32[128,128]{1,0:T(8,128)S(1)} custom-call(f32[128,128]{1,0:T(8,128)S(1)} %fusion.78), custom_call_target="Cholesky" | custom-call | tf_op jit(solution)/shard_map/jit(cholesky)/cholesky | solution.py:30
  341.0 9.8 %custom-call.32 = f32[1,128,128]{1,2,0:T(8,128)S(1)} custom-call(f32[1,128,128]{2,1,0:T(8,128)S(1)} %select_bitcast_fusion.13), custom_call_target="InvertDiagBlocksLowerTriangular" | custom-call | tf_op jit(solution)/shard_map/jit(_solve_triangular)/triangular_solve | solution.py:31
  351.6 11.7 %cholesky.435 = f32[128,128]{1,0:T(8,128)S(1)} custom-call(f32[128,128]{1,0:T(8,128)S(1)} %fusion.76), custom_call_target="Cholesky" | custom-call | tf_op jit(solution)/shard_map/jit(cholesky)/cholesky | solution.py:30
  366.2 10.0 %custom-call.41 = f32[1,128,128]{1,2,0:T(8,128)S(1)} custom-call(f32[1,128,128]{2,1,0:T(8,128)S(1)} %select_bitcast_fusion.4), custom_call_target="InvertDiagBlocksLowerTriangular" | custom-call | tf_op jit(solution)/shard_map/jit(_solve_triangular)/triangular_solve | solution.py:31
  377.8 8.5 %collective-permute-done.5 = f32[128,128]{1,0:T(8,128)S(1)} collective-permute-done((f32[128,128]{1,0:T(8,128)S(1)}, f32[128,128]{1,0:T(8,128)S(1)}, u32[]{:S(2)}, u32[]{:S(2)}) %collective-permute-start.5) | collective-permute-done | bytes 65568 | tf_op jit(solution)/shard_map/ppermute | solution.py:12
  386.7 11.7 %cholesky.446 = f32[128,128]{1,0:T(8,128)S(1)} custom-call(f32[128,128]{1,0:T(8,128)S(1)} %fusion.75), custom_call_target="Cholesky" | custom-call | tf_op jit(solution)/shard_map/jit(cholesky)/cholesky | solution.py:30
  399.8 9.8 %custom-call.33 = f32[1,128,128]{1,2,0:T(8,128)S(1)} custom-call(f32[1,128,128]{2,1,0:T(8,128)S(1)} %select_bitcast_fusion.12), custom_call_target="InvertDiagBlocksLowerTriangular" | custom-call | tf_op jit(solution)/shard_map/jit(_solve_triangular)/triangular_solve | solution.py:31
  410.3 11.7 %cholesky.457 = f32[128,128]{1,0:T(8,128)S(1)} custom-call(f32[128,128]{1,0:T(8,128)S(1)} %fusion.73), custom_call_target="Cholesky" | custom-call | tf_op jit(solution)/shard_map/jit(cholesky)/cholesky | solution.py:30
  425.0 10.2 %custom-call.40 = f32[1,128,128]{1,2,0:T(8,128)S(1)} custom-call(f32[1,128,128]{2,1,0:T(8,128)S(1)} %select_bitcast_fusion.5), custom_call_target="InvertDiagBlocksLowerTriangular" | custom-call | tf_op jit(solution)/shard_map/jit(_solve_triangular)/triangular_solve | solution.py:31
  438.8 11.7 %cholesky.468 = f32[128,128]{1,0:T(8,128)S(1)} custom-call(f32[128,128]{1,0:T(8,128)S(1)} %fusion.72), custom_call_target="Cholesky" | custom-call | tf_op jit(solution)/shard_map/jit(cholesky)/cholesky | solution.py:30
  451.9 9.8 %custom-call.34 = f32[1,128,128]{1,2,0:T(8,128)S(1)} custom-call(f32[1,128,128]{2,1,0:T(8,128)S(1)} %select_bitcast_fusion.11), custom_call_target="InvertDiagBlocksLowerTriangular" | custom-call | tf_op jit(solution)/shard_map/jit(_solve_triangular)/triangular_solve | solution.py:31
  462.4 11.7 %cholesky.479 = f32[128,128]{1,0:T(8,128)S(1)} custom-call(f32[128,128]{1,0:T(8,128)S(1)} %fusion.70), custom_call_target="Cholesky" | custom-call | tf_op jit(solution)/shard_map/jit(cholesky)/cholesky | solution.py:30
  477.0 10.0 %custom-call.39 = f32[1,128,128]{1,2,0:T(8,128)S(1)} custom-call(f32[1,128,128]{2,1,0:T(8,128)S(1)} %select_bitcast_fusion.6), custom_call_target="InvertDiagBlocksLowerTriangular" | custom-call | tf_op jit(solution)/shard_map/jit(_solve_triangular)/triangular_solve | solution.py:31
  493.8 11.7 %cholesky.490 = f32[128,128]{1,0:T(8,128)S(1)} custom-call(f32[128,128]{1,0:T(8,128)S(1)} %fusion.69), custom_call_target="Cholesky" | custom-call | tf_op jit(solution)/shard_map/jit(cholesky)/cholesky | solution.py:30
  506.9 9.8 %custom-call.35 = f32[1,128,128]{1,2,0:T(8,128)S(1)} custom-call(f32[1,128,128]{2,1,0:T(8,128)S(1)} %select_bitcast_fusion.10), custom_call_target="InvertDiagBlocksLowerTriangular" | custom-call | tf_op jit(solution)/shard_map/jit(_solve_triangular)/triangular_solve | solution.py:31
  517.4 11.7 %cholesky.501 = f32[128,128]{1,0:T(8,128)S(1)} custom-call(f32[128,128]{1,0:T(8,128)S(1)} %fusion.67), custom_call_target="Cholesky" | custom-call | tf_op jit(solution)/shard_map/jit(cholesky)/cholesky | solution.py:30
  532.1 10.0 %custom-call.38 = f32[1,128,128]{1,2,0:T(8,128)S(1)} custom-call(f32[1,128,128]{2,1,0:T(8,128)S(1)} %select_bitcast_fusion.7), custom_call_target="InvertDiagBlocksLowerTriangular" | custom-call | tf_op jit(solution)/shard_map/jit(_solve_triangular)/triangular_solve | solution.py:31
  543.7 6.7 collective-permute-done.8
  550.9 11.7 %cholesky.512 = f32[128,128]{1,0:T(8,128)S(1)} custom-call(f32[128,128]{1,0:T(8,128)S(1)} %fusion.66), custom_call_target="Cholesky" | custom-call | tf_op jit(solution)/shard_map/jit(cholesky)/cholesky | solution.py:30
  563.9 9.8 %custom-call.36 = f32[1,128,128]{1,2,0:T(8,128)S(1)} custom-call(f32[1,128,128]{2,1,0:T(8,128)S(1)} %select_bitcast_fusion.9), custom_call_target="InvertDiagBlocksLowerTriangular" | custom-call | tf_op jit(solution)/shard_map/jit(_solve_triangular)/triangular_solve | solution.py:31
  574.5 11.7 %cholesky.523 = f32[128,128]{1,0:T(8,128)S(1)} custom-call(f32[128,128]{1,0:T(8,128)S(1)} %fusion.64), custom_call_target="Cholesky" | custom-call | tf_op jit(solution)/shard_map/jit(cholesky)/cholesky | solution.py:30
  589.1 10.0 %custom-call.37 = f32[1,128,128]{1,2,0:T(8,128)S(1)} custom-call(f32[1,128,128]{2,1,0:T(8,128)S(1)} %select_bitcast_fusion.8), custom_call_target="InvertDiagBlocksLowerTriangular" | custom-call | tf_op jit(solution)/shard_map/jit(_solve_triangular)/triangular_solve | solution.py:31
  622.6 6.0 collective-permute-start.13
  647.4 6.5 collective-permute-start.24
  659.6 6.4 collective-permute-start.25
  (227 shorter events, 162.5 us)
Async XLA Ops:
  0.6 34.6 %all-to-all-start = ((f32[2,64,1024]{2,0,1:T(2,128)}), f32[2,64,1024]{2,0,1:T(2,128)S(1)}, u32[]{:S(2)}, u32[]{:S(2)}) async-start(f32[2,64,1024]{2,0,1:T(2,128)} %bitcast.268), calls=%async_computation | async-start | bytes 1048576 | tf_op jit(solution)/shard_map/all_to_all | solution.py:106
  85.1 6.2 collective-permute-start
  149.6 7.1 %collective-permute-start.1 = (f32[128,128]{1,0:T(8,128)S(1)}, f32[128,128]{1,0:T(8,128)S(1)}, u32[]{:S(2)}, u32[]{:S(2)}) collective-permute-start(f32[128,128]{1,0:T(8,128)S(1)} %fusion.109), channel_id=1, source_target_pairs={{16,0},{24,8},{32,16},{40,24},{48,32},{56,40},{64,48},{72,56},{80,... | collective-permute-start | bytes 196616 | tf_op jit(solution)/shard_map/ppermute | solution.py:12
  205.6 10.1 %collective-permute-start.2 = (f32[128,128]{1,0:T(8,128)S(1)}, f32[128,128]{1,0:T(8,128)S(1)}, u32[]{:S(2)}, u32[]{:S(2)}) collective-permute-start(f32[128,128]{1,0:T(8,128)S(1)} %fusion.110), channel_id=1, source_target_pairs={{32,0},{40,8},{48,16},{56,24},{64,32},{72,40},{80,48},{88,56},{96,... | collective-permute-start | bytes 196616 | tf_op jit(solution)/shard_map/ppermute | solution.py:12
  264.4 6.8 collective-permute-start.3
  320.1 7.4 %collective-permute-start.4 = (f32[128,128]{1,0:T(8,128)S(1)}, f32[128,128]{1,0:T(8,128)S(1)}, u32[]{:S(2)}, u32[]{:S(2)}) collective-permute-start(f32[128,128]{1,0:T(8,128)S(1)} %fusion.112), channel_id=1, source_target_pairs={{128,0},{136,8},{144,16},{152,24},{160,32},{168,40},{176,48},{184,... | collective-permute-start | bytes 196616 | tf_op jit(solution)/shard_map/ppermute | solution.py:12
  376.2 10.1 %collective-permute-start.5 = (f32[128,128]{1,0:T(8,128)S(1)}, f32[128,128]{1,0:T(8,128)S(1)}, u32[]{:S(2)}, u32[]{:S(2)}) collective-permute-start(f32[128,128]{1,0:T(8,128)S(1)} %fusion.113), channel_id=1, source_target_pairs={{256,0},{264,8},{272,16},{280,24},{288,32},{296,40},{304,48},{312,... | collective-permute-start | bytes 196616 | tf_op jit(solution)/shard_map/ppermute | solution.py:12
  435.2 3.1 collective-permute-start.6
  487.0 6.3 collective-permute-start.7
  542.1 8.3 %collective-permute-start.8 = (f32[128,128]{1,0:T(8,128)S(1)}, f32[128,128]{1,0:T(8,128)S(1)}, u32[]{:S(2)}, u32[]{:S(2)}) collective-permute-start(f32[128,128]{1,0:T(8,128)S(1)} %fusion.116), channel_id=1, source_target_pairs={{4,0},{5,1},{6,2},{7,3},{12,8},{13,9},{14,10},{15,11},{20,16},{21,... | collective-permute-start | bytes 196616 | tf_op jit(solution)/shard_map/ppermute | solution.py:12
  599.7 3.3 collective-permute-start.9
  601.3 5.7 collective-permute-start.18
  603.2 7.7 %collective-permute-start.10 = (f32[128,128]{1,0:T(8,128)S(1)}, f32[128,128]{1,0:T(8,128)S(1)}, u32[]{:S(2)}, u32[]{:S(2)}) collective-permute-start(f32[128,128]{1,0:T(8,128)S(1)} %fusion.39), channel_id=1, source_target_pairs={{0,2},{1,3},{2,4},{3,5},{4,6},{5,7},{8,10},{9,11},{10,12},{11,13},... | collective-permute-start | bytes 196616 | tf_op jit(solution)/shard_map/ppermute | solution.py:12
  607.0 5.7 collective-permute-start.19
  611.3 6.6 collective-permute-start.11
  612.8 7.2 %collective-permute-start.20 = (f32[128,128]{1,0:T(8,128)S(1)}, f32[128,128]{1,0:T(8,128)S(1)}, u32[]{:S(2)}, u32[]{:S(2)}) collective-permute-start(f32[128,128]{1,0:T(8,128)S(1)} %broadcast_select_fusion.6), channel_id=1, source_target_pairs={{0,1},{1,2},{2,3},{3,4},{4,5},{5,6},{6,7},{8,9},{9,10},{10,11},{11... | collective-permute-start | bytes 196616 | tf_op jit(solution)/shard_map/ppermute | solution.py:12
  618.4 3.8 collective-permute-start.12
  620.0 8.6 %collective-permute-start.21 = (f32[128,128]{1,0:T(8,128)S(1)}, f32[128,128]{1,0:T(8,128)S(1)}, u32[]{:S(2)}, u32[]{:S(2)}) collective-permute-start(f32[128,128]{1,0:T(8,128)S(1)} %broadcast_select_fusion.5), channel_id=1, source_target_pairs={{0,256},{8,264},{16,272},{24,280},{32,288},{40,296},{48,304},{56,3... | collective-permute-start | bytes 196616 | tf_op jit(solution)/shard_map/ppermute | solution.py:12
  622.6 10.8 %collective-permute-start.13 = (f32[128,128]{1,0:T(8,128)S(1)}, f32[128,128]{1,0:T(8,128)S(1)}, u32[]{:S(2)}, u32[]{:S(2)}) collective-permute-start(f32[128,128]{1,0:T(8,128)S(1)} %fusion.30), channel_id=1, source_target_pairs={{0,128},{8,136},{16,144},{24,152},{32,160},{40,168},{48,176},{56,1... | collective-permute-start | bytes 196616 | tf_op jit(solution)/shard_map/ppermute | solution.py:12
  628.6 10.9 %collective-permute-start.22 = (f32[128,128]{1,0:T(8,128)S(1)}, f32[128,128]{1,0:T(8,128)S(1)}, u32[]{:S(2)}, u32[]{:S(2)}) collective-permute-start(f32[128,128]{1,0:T(8,128)S(1)} %broadcast_select_fusion.4), channel_id=1, source_target_pairs={{0,128},{8,136},{16,144},{24,152},{32,160},{40,168},{48,176},{56,1... | collective-permute-start | bytes 196616 | tf_op jit(solution)/shard_map/ppermute | solution.py:12
  633.8 8.5 %collective-permute-start.14 = (f32[128,128]{1,0:T(8,128)S(1)}, f32[128,128]{1,0:T(8,128)S(1)}, u32[]{:S(2)}, u32[]{:S(2)}) collective-permute-start(f32[128,128]{1,0:T(8,128)S(1)} %fusion.27), channel_id=1, source_target_pairs={{0,64},{8,72},{16,80},{24,88},{32,96},{40,104},{48,112},{56,120},{... | collective-permute-start | bytes 196616 | tf_op jit(solution)/shard_map/ppermute | solution.py:12
  639.6 7.8 %collective-permute-start.23 = (f32[128,128]{1,0:T(8,128)S(1)}, f32[128,128]{1,0:T(8,128)S(1)}, u32[]{:S(2)}, u32[]{:S(2)}) collective-permute-start(f32[128,128]{1,0:T(8,128)S(1)} %broadcast_select_fusion.3), channel_id=1, source_target_pairs={{0,64},{8,72},{16,80},{24,88},{32,96},{40,104},{48,112},{56,120},{... | collective-permute-start | bytes 196616 | tf_op jit(solution)/shard_map/ppermute | solution.py:12
  642.8 11.1 %collective-permute-start.15 = (f32[128,128]{1,0:T(8,128)S(1)}, f32[128,128]{1,0:T(8,128)S(1)}, u32[]{:S(2)}, u32[]{:S(2)}) collective-permute-start(f32[128,128]{1,0:T(8,128)S(1)} %fusion.24), channel_id=1, source_target_pairs={{0,32},{8,40},{16,48},{24,56},{32,64},{40,72},{48,80},{56,88},{64,... | collective-permute-start | bytes 196616 | tf_op jit(solution)/shard_map/ppermute | solution.py:12
  647.4 12.2 %collective-permute-start.24 = (f32[128,128]{1,0:T(8,128)S(1)}, f32[128,128]{1,0:T(8,128)S(1)}, u32[]{:S(2)}, u32[]{:S(2)}) collective-permute-start(f32[128,128]{1,0:T(8,128)S(1)} %broadcast_select_fusion.2), channel_id=1, source_target_pairs={{0,32},{8,40},{16,48},{24,56},{32,64},{40,72},{48,80},{56,88},{64,... | collective-permute-start | bytes 196616 | tf_op jit(solution)/shard_map/ppermute | solution.py:12
  654.3 11.6 %collective-permute-start.16 = (f32[128,128]{1,0:T(8,128)S(1)}, f32[128,128]{1,0:T(8,128)S(1)}, u32[]{:S(2)}, u32[]{:S(2)}) collective-permute-start(f32[128,128]{1,0:T(8,128)S(1)} %fusion.21), channel_id=1, source_target_pairs={{0,16},{8,24},{16,32},{24,40},{32,48},{40,56},{48,64},{56,72},{64,... | collective-permute-start | bytes 196616 | tf_op jit(solution)/shard_map/ppermute | solution.py:12
  659.6 12.6 %collective-permute-start.25 = (f32[128,128]{1,0:T(8,128)S(1)}, f32[128,128]{1,0:T(8,128)S(1)}, u32[]{:S(2)}, u32[]{:S(2)}) collective-permute-start(f32[128,128]{1,0:T(8,128)S(1)} %broadcast_select_fusion.1), channel_id=1, source_target_pairs={{0,16},{8,24},{16,32},{24,40},{32,48},{40,56},{48,64},{56,72},{64,... | collective-permute-start | bytes 196616 | tf_op jit(solution)/shard_map/ppermute | solution.py:12
  666.4 9.2 %collective-permute-start.17 = (f32[128,128]{1,0:T(8,128)S(1)}, f32[128,128]{1,0:T(8,128)S(1)}, u32[]{:S(2)}, u32[]{:S(2)}) collective-permute-start(f32[128,128]{1,0:T(8,128)S(1)} %fusion.18), channel_id=1, source_target_pairs={{0,8},{8,16},{16,24},{24,32},{32,40},{40,48},{48,56},{56,64},{64,7... | collective-permute-start | bytes 196616 | tf_op jit(solution)/shard_map/ppermute | solution.py:12
  672.2 8.3 %collective-permute-start.26 = (f32[128,128]{1,0:T(8,128)S(1)}, f32[128,128]{1,0:T(8,128)S(1)}, u32[]{:S(2)}, u32[]{:S(2)}) collective-permute-start(f32[128,128]{1,0:T(8,128)S(1)} %broadcast_select_fusion), channel_id=1, source_target_pairs={{0,8},{8,16},{16,24},{24,32},{32,40},{40,48},{48,56},{56,64},{64,7... | collective-permute-start | bytes 196616 | tf_op jit(solution)/shard_map/ppermute | solution.py:12
where the time goes:
time: 692 us; the launch traced here: 682 us
  other arithmetic  470 us (68%)
  starting transfers between devices  107 us (15%)
  waiting for transfers between devices  64.8 us (9%)
  matrix products  35.1 us (5%)
    another operation x60, other arithmetic, cholesky_pass(): lower_factor = jnp.linalg.cholesky(gram_matrix)  248 us
    another operation x40, other arithmetic, cholesky_pass(): jax.scipy.linalg.solve_triangular(lower_factor, columns, lower=True)  221 us
    ppermute x27, starting transfers between devices, shifted(): return lax.ppermute(block, axis, route)  90.8 us
    ppermute x27, waiting for transfers between devices, shifted(): return lax.ppermute(block, axis, route)  46.3 us
    dot_general x29, matrix products, product(): jnp.dot(left, right, precision=lax.Precision.HIGHEST, preferred_element_t...  21.2 us
    all_to_all x1, waiting for transfers between devices, shards(): lax.all_to_all(snapshots, 'wide', split_axis=1, concat_axis=0, tiled=True)  18.5 us
    all_to_all x1, starting transfers between devices, shards(): lax.all_to_all(snapshots, 'wide', split_axis=1, concat_axis=0, tiled=True)  15.8 us
  transfers between devices with their start and end apart: 28, of which 16 were waited for; matrix products, arithmetic and copies ran while one was open for 1% of the time, Pallas kernels for 0%

commit v1 on v0

v1 whole, which is shorter than its diff:
```python
import math

import jax
import jax.numpy as jnp
from jax import lax
from jax.sharding import PartitionSpec as P

LIMIT = 4096.0


def product(left, right, dims=((1,), (0,))):
    return lax.dot_general(
        left,
        right,
        (dims, ((), ())),
        precision=lax.Precision.HIGHEST,
        preferred_element_type=jnp.float32,
    )


def side_groups(size, side):
    near = [[far * side + step for step in range(side)] for far in range(size // side)]
    across = [[far * side + step for far in range(size // side)] for step in range(side)]
    return near, across


def total(partial):
    near, across = side_groups(lax.axis_size("wide"), 8)
    partial = jnp.sum(lax.all_gather(partial, "narrow"), axis=0)
    partial = jnp.sum(lax.all_gather(partial, "wide", axis_index_groups=near), axis=0)
    return jnp.sum(lax.all_gather(partial, "wide", axis_index_groups=across), axis=0)


def factor(gram):
    lower = jnp.linalg.cholesky(gram)
    eye = jnp.eye(gram.shape[0], dtype=jnp.float32)
    inverse = jax.scipy.linalg.solve_triangular(lower, eye, lower=True)
    spread = jnp.sum(inverse * inverse * jnp.diagonal(gram)[None, :])
    return lower, inverse, spread


def shards(snapshots):
    held, length = snapshots.shape
    groups = lax.axis_size("wide")
    lanes = 128
    pieces = length // groups // lanes
    blocks = snapshots.reshape(held, groups, pieces, lanes).transpose(1, 2, 0, 3)
    blocks = blocks.reshape(groups, pieces * held, lanes)
    blocks = lax.all_to_all(blocks, "wide", split_axis=0, concat_axis=0, tiled=True)
    blocks = blocks.reshape(groups, pieces, held, lanes).transpose(0, 2, 1, 3)
    columns = blocks.reshape(groups * held, pieces * lanes)

    lower, inverse, spread = factor(total(product(columns, columns, ((1,), (1,)))))

    def rough(state):
        step, _, _, spread = state
        return jnp.logical_and(step < 4, jnp.logical_not(spread <= LIMIT))

    def again(state):
        step, inverse, upper, _ = state
        rows = product(inverse, columns)
        lower, more, spread = factor(total(product(rows, rows, ((1,), (1,)))))
        return step + 1, product(more, inverse), product(lower, upper, ((0,), (0,))), spread

    state = (jnp.int32(0), inverse, jnp.transpose(lower), spread)
    _, inverse, upper, _ = lax.while_loop(rough, again, state)
    rows_total = length * lax.axis_size("narrow")
    root = math.sqrt(rows_total)
    return product(columns, inverse * root, ((0,), (1,))), upper / root


def solution(mesh):
    in_specs = (P("wide", "narrow"),)
    out_specs = (P(("narrow", "wide"), None), P())
    return jax.shard_map(shards, mesh=mesh, in_specs=in_specs, out_specs=out_specs, check_vma=False)
```

time: 692 us -> 133 us (0.19)
  the two profiles are of different devices: /device:TPU:64 before, /device:TPU:2 now
where the time goes in v1:
time: 133 us
  blocking collectives  63.9 us (48%)
  other arithmetic  23.6 us (18%)
  waiting for transfers between devices  19.7 us (15%)
  starting transfers between devices  16.6 us (12%)
  local copies, waits for them, and re-layouts  5.27 us (4%)
  matrix products  2.17 us (2%)
    all_gather x1, blocking collectives, total(): lax.all_gather(partial, 'wide', axis_index_groups=across)  25.4 us
    all_gather x1, blocking collectives, total(): lax.all_gather(partial, 'wide', axis_index_groups=near)  25.3 us
    all_to_all x1, waiting for transfers between devices, shards(): lax.all_to_all(blocks, 'wide', split_axis=0, concat_axis=0, tiled=True)  19.7 us
    all_to_all x1, starting transfers between devices, shards(): lax.all_to_all(blocks, 'wide', split_axis=0, concat_axis=0, tiled=True)  16.6 us
    all_gather x1, blocking collectives, total(): partial = jnp.sum(lax.all_gather(partial, 'narrow'), axis=0)  13.2 us
    another operation x3, other arithmetic, factor(): lower = jnp.linalg.cholesky(gram)  12.4 us
    another operation x1, other arithmetic, factor(): inverse = jax.scipy.linalg.solve_triangular(lower, eye, lower=True)  9.81 us
  transfers between devices with their start and end apart: 1, of which 1 were waited for; matrix products, arithmetic and copies ran while one was open for 0% of the time, Pallas kernels for 0%

profile of v1, /device:TPU:2, one launch (start us, length us, event | category | flops | bytes accessed | tf_op | source)
XLA Modules:
  0.0 132.8 jit_solution(1537192321191527217)
XLA Ops:
  0.6 1.1 copy.50
  1.7 0.1 copy.36
  1.8 1.1 copy.37
  2.9 16.6 %all-to-all-start = ((f32[64,16,128]{2,1,0:T(8,128)}), f32[64,16,128]{2,1,0:T(8,128)S(1)}, u32[]{:S(2)}, u32[]{:S(2)}) async-start(f32[64,16,128]{2,1,0:T(8,128)} %copy.37), calls=%async_computation | async-start | bytes 1048576 | tf_op jit(solution)/shard_map/all_to_all | solution.py:49
  19.5 19.7 %all-to-all-done = f32[64,16,128]{2,1,0:T(8,128)S(1)} async-done(((f32[64,16,128]{2,1,0:T(8,128)}), f32[64,16,128]{2,1,0:T(8,128)S(1)}, u32[]{:S(2)}, u32[]{:S(2)}) %all-to-all-start) | async-done | bytes 524320 | tf_op jit(solution)/shard_map/all_to_all | solution.py:49
  39.2 0.2 copy.38
  39.4 0.3 copy.39
  39.7 0.6 fusion.23
  40.4 0.1 copy.49
  40.5 13.2 %all-gather.3 = f32[1024,128]{1,0:T(8,128)S(1)} all-gather(f32[128,128]{1,0:T(8,128)S(1)} %fusion.23), channel_id=5, replica_groups=mesh['wide'=64,'narrow'=8] {'narrow'}, dimensions={0}, use_global_device_ids=true | all-gather | bytes 589824 | tf_op jit(solution)/shard_map/all_gather | solution.py:29
  53.7 25.3 %all-gather.4 = f32[1024,128]{1,0:T(8,128)S(1)} all-gather(f32[128,128]{1,0:T(8,128)S(1)} %reduce_sum.72), channel_id=6, replica_groups={{0,8,16,24,32,40,48,56},{64,72,80,88,96,104,112,120},{128,136,144,152,1..., dimensions={0}, use_global_device_ids=true | all-gather | bytes 589824 | tf_op jit(solution)/shard_map/all_gather | solution.py:30
  79.0 25.4 %all-gather.5 = f32[1024,128]{1,0:T(8,128)S(1)} all-gather(f32[128,128]{1,0:T(8,128)S(1)} %reduce_sum.73), channel_id=7, replica_groups={{0,64,128,192,256,320,384,448},{8,72,136,200,264,328,392,456},{16,80,14..., dimensions={0}, use_global_device_ids=true | all-gather | bytes 589824 | tf_op jit(solution)/shard_map/all_gather | solution.py:31
  104.4 0.1 copy.40
  104.6 11.7 %custom-call.14 = f32[128,128]{1,0:T(8,128)S(1)} custom-call(f32[128,128]{1,0:T(8,128)S(1)} %fusion.15), custom_call_target="Cholesky" | custom-call | tf_op jit(solution)/shard_map/jit(cholesky)/cholesky/custom-call.1 | solution.py:35
  116.3 0.6 compare_reduce_fusion.1
  116.9 0.7 fusion.20
  117.6 9.8 %custom-call.15 = f32[1,128,128]{1,2,0:T(8,128)S(1)} custom-call(f32[1,128,128]{2,1,0:T(8,128)S(1)} %get-tuple-element.89), custom_call_target="InvertDiagBlocksLowerTriangular" | custom-call | tf_op jit(solution)/shard_map/jit(_solve_triangular)/triangular_solve/custom-call.0 | solution.py:37
  127.4 1.2 gather_fusion.1
  128.7 0.1 copy.41
  128.8 0.9 multiply_reduce_fusion.1
  129.7 0.8 while.14
  130.5 0.7 convolution_bitcast_fusion
  131.2 1.0 copy.42
  132.2 0.6 broadcast_multiply_fusion
  (6 shorter events, 0.1 us)
Async XLA Ops:
  2.9 36.3 %all-to-all-start = ((f32[64,16,128]{2,1,0:T(8,128)}), f32[64,16,128]{2,1,0:T(8,128)S(1)}, u32[]{:S(2)}, u32[]{:S(2)}) async-start(f32[64,16,128]{2,1,0:T(8,128)} %copy.37), calls=%async_computation | async-start | bytes 1048576 | tf_op jit(solution)/shard_map/all_to_all | solution.py:49

commit v2 on v1

v2 whole, which is shorter than its diff:
```python
import math

import jax
import jax.numpy as jnp
from jax import lax
from jax.experimental import pallas as pl
from jax.experimental.pallas import tpu as pltpu
from jax.sharding import PartitionSpec as P

LANES = 128
SUBLANES = 8
PANEL = 16
FLOOR = 1e-6
LIMIT = 4096.0
PASSES = 5


def product(left, right, dims=((1,), (0,))):
    return lax.dot_general(
        left,
        right,
        (dims, ((), ())),
        precision=lax.Precision.HIGHEST,
        preferred_element_type=jnp.float32,
    )


def side_groups(size, side):
    near = [[far * side + step for step in range(side)] for far in range(size // side)]
    across = [[far * side + step for far in range(size // side)] for step in range(side)]
    return near, across


def exchange(pieces, axis, groups=None):
    return lax.all_to_all(
        pieces, axis, split_axis=0, concat_axis=0, axis_index_groups=groups, tiled=True
    )


def total(partial):
    order = partial.shape[0]
    slabs = lax.axis_size("narrow")
    size = lax.axis_size("wide")
    side = math.isqrt(size)
    near, across = side_groups(size, side)
    slab = jnp.sum(exchange(partial.reshape(slabs, order // slabs, order), "narrow"), axis=0)
    slab = jnp.sum(exchange(jnp.broadcast_to(slab, (side, *slab.shape)), "wide", near), axis=0)
    slab = jnp.sum(exchange(jnp.broadcast_to(slab, (side, *slab.shape)), "wide", across), axis=0)
    slab = jnp.broadcast_to(slab, (slabs, *slab.shape))
    return exchange(slab, "narrow").reshape(order, order)


def split(value):
    high = value.astype(jnp.bfloat16)
    rest = value - high.astype(jnp.float32)
    middle = rest.astype(jnp.bfloat16)
    low = (rest - middle.astype(jnp.float32)).astype(jnp.bfloat16)
    return high, middle, low


def replicated(value):
    return jnp.broadcast_to(value, (SUBLANES, LANES))


def stacked(values):
    place = lax.broadcasted_iota(jnp.int32, (SUBLANES, LANES), 0)
    blocks = []
    for first in range(0, len(values), SUBLANES):
        block = values[first]
        for step in range(1, SUBLANES):
            block = jnp.where(place == step, values[first + step], block)
        blocks.append(block)
    return jnp.concatenate(blocks, axis=0)


def factor_kernel(gram_ref, inverse_ref, upper_ref, spread_ref, work):
    order = gram_ref.shape[0]
    gram = gram_ref[...]
    across = lax.broadcasted_iota(jnp.int32, (order, order), 1)
    down = lax.broadcasted_iota(jnp.int32, (order, order), 0)
    diagonal = jnp.where(across == down, gram, 0.0)
    scale = lax.rsqrt(jnp.sum(diagonal, axis=0, keepdims=True))
    work[:, :order] = gram * scale * lax.rsqrt(jnp.sum(diagonal, axis=1, keepdims=True))
    work[:, order:] = jnp.where(across == down, 1.0, 0.0)
    for base in range(0, order, PANEL):
        end = base + PANEL
        panel = work[base:end, base:end]
        entry = {}
        for col in range(PANEL):
            spread_col = jnp.broadcast_to(panel[:, col : col + 1], (PANEL, LANES))
            for row in range(col + 1):
                entry[row, col] = replicated(spread_col[row : row + 1, :])
        left = [replicated(work[base + row : base + row + 1, :order]) for row in range(PANEL)]
        right = [replicated(work[base + row : base + row + 1, order:]) for row in range(PANEL)]
        for pivot in range(PANEL):
            inv = lax.rsqrt(jnp.maximum(entry[pivot, pivot], FLOOR))
            left[pivot] = left[pivot] * inv
            right[pivot] = right[pivot] * inv
            for col in range(pivot + 1, PANEL):
                entry[pivot, col] = entry[pivot, col] * inv
            for col in range(pivot + 1, PANEL):
                ratio = entry[pivot, col]
                for row in range(pivot + 1, col + 1):
                    entry[row, col] = entry[row, col] - entry[pivot, row] * ratio
                left[col] = left[col] - ratio * left[pivot]
                right[col] = right[col] - ratio * right[pivot]
        rows = jnp.concatenate([stacked(left), stacked(right)], axis=1)
        work[base:end, :] = rows
        if end < order:
            high, middle, low = split(rows)
            first = jnp.concatenate([high, high, middle, high, low, middle], axis=0)
            second = jnp.concatenate([high, middle, high, low, high, middle], axis=0)
            update = lax.dot_general(
                first[:, :order],
                second,
                (((0,), (0,)), ((), ())),
                preferred_element_type=jnp.float32,
            )
            work[end:, :] -= update[end:, :]
    inverse = jnp.where(across <= down, work[:, order:], 0.0)
    spread_ref[...] = jnp.full(spread_ref.shape, jnp.sum(inverse * inverse))
    inverse_ref[...] = inverse * scale
    upper_ref[...] = jnp.where(across >= down, work[:, :order], 0.0) * (1.0 / scale)


def factor(gram):
    order = gram.shape[0]
    square = jax.ShapeDtypeStruct((order, order), jnp.float32)
    whole = pl.BlockSpec(memory_space=pltpu.VMEM)
    inverse, upper, spread = pl.pallas_call(
        factor_kernel,
        out_shape=[square, square, jax.ShapeDtypeStruct((SUBLANES, LANES), jnp.float32)],
        in_specs=[whole],
        out_specs=[whole] * 3,
        scratch_shapes=[pltpu.VMEM((order, 2 * order), jnp.float32)],
        name="factor",
    )(gram)
    return inverse, upper, spread[0, 0]


def shards(snapshots):
    held, length = snapshots.shape
    groups = lax.axis_size("wide")
    tiles = length // LANES
    blocks = snapshots.reshape(held, tiles, LANES).transpose(1, 0, 2)
    blocks = exchange(blocks, "wide").reshape(groups, tiles // groups, held, LANES)
    columns = blocks.transpose(0, 2, 1, 3).reshape(groups * held, length // groups)

    inverse, upper, spread = factor(total(product(columns, columns, ((1,), (1,)))))

    def rough(state):
        step, _, _, spread = state
        return jnp.logical_and(step < PASSES, jnp.logical_not(spread <= LIMIT))

    def again(state):
        step, inverse, upper, _ = state
        rows = product(inverse, columns)
        more, next_upper, spread = factor(total(product(rows, rows, ((1,), (1,)))))
        return step + 1, product(more, inverse), product(next_upper, upper), spread

    _, inverse, upper, _ = lax.while_loop(rough, again, (jnp.int32(1), inverse, upper, spread))
    root = math.sqrt(length * lax.axis_size("narrow"))
    return product(columns, inverse * root, ((0,), (1,))), upper / root


def solution(mesh):
    in_specs = (P("wide", "narrow"),)
    out_specs = (P(("narrow", "wide"), None), P())
    return jax.shard_map(shards, mesh=mesh, in_specs=in_specs, out_specs=out_specs, check_vma=False)
```

time: 133 us -> 92.1 us (0.69)
  the two profiles are of different devices: /device:TPU:2 before, /device:TPU:1 now
where the time goes in v2:
time: 92.1 us; the launch traced here: 91.6 us
  blocking collectives  66.7 us (72%)
  starting transfers between devices  6.6 us (7%)
  Pallas kernels  6.43 us (7%)
  waiting for transfers between devices  4.77 us (5%)
  local copies, waits for them, and re-layouts  3.8 us (4%)
  matrix products  1.24 us (1%)
    all_to_all x4, blocking collectives, exchange(): lax.all_to_all(pieces, axis, split_axis=0, concat_axis=0, axis_index_grou...  66.7 us
    all_to_all x1, starting transfers between devices, exchange(): lax.all_to_all(pieces, axis, split_axis=0, concat_axis=0, axis_index_grou...  6.6 us
    pallas_call x1, Pallas kernels, factor(): pl.pallas_call(factor_kernel, out_shape=[square, square, jax.ShapeDtypeSt...  6.43 us
    all_to_all x1, waiting for transfers between devices, exchange(): lax.all_to_all(pieces, axis, split_axis=0, concat_axis=0, axis_index_grou...  4.77 us
  transfers between devices with their start and end apart: 1, of which 1 were waited for; matrix products, arithmetic and copies ran while one was open for 0% of the time, Pallas kernels for 0%

profile of v2, /device:TPU:1, one launch (start us, length us, event | category | flops | bytes accessed | tf_op | source)
XLA Modules:
  0.0 91.6 jit_solution(14618270383449156182)
XLA Ops:
  0.6 34.3 %all_to_all.49 = f32[512,2,128]{2,1,0:T(2,128)S(1)} all-to-all(f32[512,2,128]{2,1,0:T(2,128)} %bitcast.63), channel_id=1, replica_groups=mesh['wide'=64,'narrow'=8] {'wide'}, dimensions={0} | all-to-all | bytes 1048576 | tf_op jit(solution)/shard_map/all_to_all | solution.py:35
  35.0 0.1 dot_general.22
  35.1 0.1 reshape.29
  35.2 0.6 fusion.7
  35.8 12.4 %all_to_all.50 = f32[8,16,128]{2,1,0:T(8,128)S(1)} all-to-all(f32[8,16,128]{2,1,0:T(8,128)S(1)} %fusion.7), channel_id=1, replica_groups=mesh['wide'=64,'narrow'=8] {'narrow'}, dimensions={0} | all-to-all | bytes 131072 | tf_op jit(solution)/shard_map/all_to_all | solution.py:35
  48.3 10.4 %all_to_all.51 = f32[8,16,128]{2,1,0:T(8,128)S(1)} all-to-all(f32[8,16,128]{2,1,0:T(8,128)S(1)} %broadcast_in_dim.18), channel_id=1, replica_groups={{0,8,16,24,32,40,48,56},{64,72,80,88,96,104,112,120},{128,136,144,152,1..., dimensions={0} | all-to-all | bytes 131072 | tf_op jit(solution)/shard_map/all_to_all | solution.py:35
  58.7 9.6 %all_to_all.52 = f32[8,16,128]{2,1,0:T(8,128)S(1)} all-to-all(f32[8,16,128]{2,1,0:T(8,128)S(1)} %broadcast_in_dim.19), channel_id=1, replica_groups={{0,64,128,192,256,320,384,448},{8,72,136,200,264,328,392,456},{16,80,14..., dimensions={0} | all-to-all | bytes 131072 | tf_op jit(solution)/shard_map/all_to_all | solution.py:35
  68.3 0.6 broadcast_in_dim.20
  68.9 6.6 %all-to-all-start.8 = ((f32[8,16,128]{2,1,0:T(8,128)}), f32[8,16,128]{2,1,0:T(8,128)S(1)}, u32[]{:S(2)}, u32[]{:S(2)}) async-start(f32[8,16,128]{2,1,0:T(8,128)} %broadcast_in_dim.20), calls=%async_computation.8 | async-start | bytes 131072 | tf_op jit(solution)/shard_map/all_to_all | solution.py:35
  75.5 0.1 copy.19
  75.6 4.8 %all-to-all-done.8 = f32[8,16,128]{2,1,0:T(8,128)S(1)} async-done(((f32[8,16,128]{2,1,0:T(8,128)}), f32[8,16,128]{2,1,0:T(8,128)S(1)}, u32[]{:S(2)}, u32[]{:S(2)}) %all-to-all-start.8) | async-done | bytes 65568 | tf_op jit(solution)/shard_map/all_to_all | solution.py:35
  80.4 0.0 copy-start.2
  80.4 0.6 copy-done.2
  81.0 6.4 %factor.2 = (f32[128,128]{1,0:T(8,128)S(1)}, f32[128,128]{1,0:T(8,128)S(1)}, f32[8,128]{1,0:T(8,128)}) custom-call(f32[128,128]{1,0:T(8,128)} %bitcast.64), custom_call_target="tpu_custom_call" | custom-call | tf_op jit(solution)/shard_map/factor/pallas_call | solution.py:130
  87.5 1.2 %slice.6 = f32[1,1]{1,0:T(1,128)} slice(f32[8,128]{1,0:T(8,128)} %get-tuple-element.38), slice={[0:1], [0:1]} | slice | bytes 8 | tf_op jit(solution)/shard_map/slice | solution.py:138
  88.7 0.7 while.14
  89.3 0.7 convolution_bitcast_fusion
  90.0 1.0 %copy.14 = f32[1024,128]{1,0:T(8,128)} copy(f32[1024,128]{0,1:T(8,128)S(1)} %convolution_bitcast_fusion) | data formatting | bytes 1048576
  91.0 0.6 broadcast_multiply_fusion
  (7 shorter events, 0.1 us)
Async XLA Ops:
  68.9 11.5 %all-to-all-start.8 = ((f32[8,16,128]{2,1,0:T(8,128)}), f32[8,16,128]{2,1,0:T(8,128)S(1)}, u32[]{:S(2)}, u32[]{:S(2)}) async-start(f32[8,16,128]{2,1,0:T(8,128)} %broadcast_in_dim.20), calls=%async_computation.8 | async-start | bytes 131072 | tf_op jit(solution)/shard_map/all_to_all | solution.py:35
  80.4 0.6 copy-start.2

commit v3 on v2

--- a/solution.py
+++ b/solution.py
@@ -1,3 +1,4 @@
+import functools
 import math
 
 import jax
@@ -25,29 +26,64 @@
     )
 
 
-def side_groups(size, side):
-    near = [[far * side + step for step in range(side)] for far in range(size // side)]
-    across = [[far * side + step for far in range(size // side)] for step in range(side)]
-    return near, across
-
-
 def exchange(pieces, axis, groups=None):
     return lax.all_to_all(
         pieces, axis, split_axis=0, concat_axis=0, axis_index_groups=groups, tiled=True
     )
 
 
-def total(partial):
-    order = partial.shape[0]
-    slabs = lax.axis_size("narrow")
-    size = lax.axis_size("wide")
-    side = math.isqrt(size)
-    near, across = side_groups(size, side)
-    slab = jnp.sum(exchange(partial.reshape(slabs, order // slabs, order), "narrow"), axis=0)
-    slab = jnp.sum(exchange(jnp.broadcast_to(slab, (side, *slab.shape)), "wide", near), axis=0)
-    slab = jnp.sum(exchange(jnp.broadcast_to(slab, (side, *slab.shape)), "wide", across), axis=0)
-    slab = jnp.broadcast_to(slab, (slabs, *slab.shape))
-    return exchange(slab, "narrow").reshape(order, order)
+def members(axis, stride, count):
+    size = lax.axis_size(axis)
+    return [
+        [first + step * stride for step in range(count)]
+        for block in range(0, size, stride * count)
+        for first in range(block, block + stride)
+    ]
+
+
+def added(part, axis, stride, count):
+    pieces = jnp.broadcast_to(part, (count, *part.shape))
+    return jnp.sum(exchange(pieces, axis, members(axis, stride, count)), axis=0)
+
+
+def paired(part):
+    return lax.all_gather(part, "narrow", axis_index_groups=members("narrow", 1, 2))
+
+
+def total(packed):
+    half = packed.shape[0] // 2
+    both = jnp.sum(paired(packed), axis=0)
+    part = lax.dynamic_slice_in_dim(both, lax.axis_index("narrow") % 2 * half, half, axis=0)
+    side = math.isqrt(lax.axis_size("wide"))
+    part = added(part, "narrow", 2, lax.axis_size("narrow") // 2)
+    part = added(part, "wide", 1, side)
+    part = added(part, "wide", side, lax.axis_size("wide") // side)
+    return paired(part).reshape(packed.shape)
+
+
+def gram_kernel(columns_ref, packed_ref):
+    columns = columns_ref[...]
+    gram = product(columns, columns, ((1,), (1,)))
+    half = gram.shape[0] // 2
+    across = lax.broadcasted_iota(jnp.int32, (half, 2 * half), 1)
+    down = lax.broadcasted_iota(jnp.int32, (half, 2 * half), 0)
+    bottom = gram[half:, :]
+    packed_ref[:half, :] = jnp.where(across < down, pltpu.roll(bottom, half, 1), gram[:half, :])
+    corner = jnp.sum(jnp.where(across == down + half, bottom, 0.0), axis=0, keepdims=True)
+    rest = packed_ref.shape[0] - half
+    packed_ref[half:, :] = jnp.broadcast_to(corner, (rest, 2 * half))
+
+
+def gram(columns):
+    order = columns.shape[0]
+    rows = order // 2 + 2 * SUBLANES
+    return pl.pallas_call(
+        gram_kernel,
+        out_shape=jax.ShapeDtypeStruct((rows, order), jnp.float32),
+        in_specs=[pl.BlockSpec(memory_space=pltpu.VMEM)],
+        out_specs=pl.BlockSpec(memory_space=pltpu.VMEM),
+        name="gram",
+    )(columns)
 
 
 def split(value):
@@ -73,11 +109,15 @@
     return jnp.concatenate(blocks, axis=0)
 
 
-def factor_kernel(gram_ref, inverse_ref, upper_ref, spread_ref, work):
-    order = gram_ref.shape[0]
-    gram = gram_ref[...]
+def factor_kernel(root, packed_ref, inverse_ref, upper_ref, spread_ref, work):
+    order = packed_ref.shape[1]
+    half = order // 2
     across = lax.broadcasted_iota(jnp.int32, (order, order), 1)
     down = lax.broadcasted_iota(jnp.int32, (order, order), 0)
+    top = packed_ref[:half, :]
+    flipped = pltpu.roll(jnp.transpose(jnp.concatenate([top, top], axis=0))[:half, :], half, 1)
+    bottom = jnp.where((across == down + half)[:half, :], packed_ref[half : half + 1, :], flipped)
+    gram = jnp.concatenate([top, bottom], axis=0)
     diagonal = jnp.where(across == down, gram, 0.0)
     scale = lax.rsqrt(jnp.sum(diagonal, axis=0, keepdims=True))
     work[:, :order] = gram * scale * lax.rsqrt(jnp.sum(diagonal, axis=1, keepdims=True))
@@ -118,24 +158,44 @@
             )
             work[end:, :] -= update[end:, :]
     inverse = jnp.where(across <= down, work[:, order:], 0.0)
-    spread_ref[...] = jnp.full(spread_ref.shape, jnp.sum(inverse * inverse))
-    inverse_ref[...] = inverse * scale
-    upper_ref[...] = jnp.where(across >= down, work[:, :order], 0.0) * (1.0 / scale)
-
-
-def factor(gram):
-    order = gram.shape[0]
+    spread_ref[...] = jnp.sum(inverse * inverse, keepdims=True)
+    inverse_ref[...] = inverse * (scale * root)
+    upper_ref[...] = jnp.where(across >= down, work[:, :order], 0.0) * (1.0 / (scale * root))
+
+
+def factor(packed, root):
+    order = packed.shape[1]
     square = jax.ShapeDtypeStruct((order, order), jnp.float32)
     whole = pl.BlockSpec(memory_space=pltpu.VMEM)
     inverse, upper, spread = pl.pallas_call(
-        factor_kernel,
-        out_shape=[square, square, jax.ShapeDtypeStruct((SUBLANES, LANES), jnp.float32)],
+        functools.partial(factor_kernel, root),
+        out_shape=[square, square, jax.ShapeDtypeStruct((1, 1), jnp.float32)],
         in_specs=[whole],
         out_specs=[whole] * 3,
         scratch_shapes=[pltpu.VMEM((order, 2 * order), jnp.float32)],
         name="factor",
-    )(gram)
-    return inverse, upper, spread[0, 0]
+    )(packed)
+    return inverse, upper, spread.reshape(())
+
+
+def apply_kernel(columns_ref, inverse_ref, rows_ref):
+    rows_ref[...] = product(columns_ref[...], inverse_ref[...], ((0,), (1,)))
+
+
+def apply(columns, inverse):
+    order, length = columns.shape
+    step = math.gcd(length, 2 * LANES)
+    return pl.pallas_call(
+        apply_kernel,
+        out_shape=jax.ShapeDtypeStruct((length, order), jnp.float32),
+        grid=(length // step,),
+        in_specs=[
+            pl.BlockSpec((order, step), lambda i: (0, i)),
+            pl.BlockSpec((order, order), lambda i: (0, 0)),
+        ],
+        out_specs=pl.BlockSpec((step, order), lambda i: (i, 0)),
+        name="apply",
+    )(columns, inverse)
 
 
 def shards(snapshots):
@@ -146,7 +206,9 @@
     blocks = exchange(blocks, "wide").reshape(groups, tiles // groups, held, LANES)
     columns = blocks.transpose(0, 2, 1, 3).reshape(groups * held, length // groups)
 
-    inverse, upper, spread = factor(total(product(columns, columns, ((1,), (1,)))))
+    root = math.sqrt(length * lax.axis_size("narrow"))
+
+    inverse, upper, spread = factor(total(gram(columns)), root)
 
     def rough(state):
         step, _, _, spread = state
@@ -154,13 +216,11 @@
 
     def again(state):
         step, inverse, upper, _ = state
-        rows = product(inverse, columns)
-        more, next_upper, spread = factor(total(product(rows, rows, ((1,), (1,)))))
+        more, next_upper, spread = factor(total(gram(product(inverse, columns))), root)
         return step + 1, product(more, inverse), product(next_upper, upper), spread
 
     _, inverse, upper, _ = lax.while_loop(rough, again, (jnp.int32(1), inverse, upper, spread))
-    root = math.sqrt(length * lax.axis_size("narrow"))
-    return product(columns, inverse * root, ((0,), (1,))), upper / root
+    return apply(columns, inverse), upper
 
 
 def solution(mesh):

time: 92.1 us -> 89.6 us (0.973)
  blocking collectives: 66.7 us -> 30.9 us
  waiting for transfers between devices: 4.77 us -> 25.4 us
  starting transfers between devices: 6.6 us -> 20.5 us
  Pallas kernels: 6.43 us -> 10 us
  local copies, waits for them, and re-layouts: 3.8 us -> 0.88 us
  matrix products: 1.24 us -> 0 us
    all_to_all x4 -> x2, blocking collectives: 66.7 us -> 19.9 us  [exchange(): lax.all_to_all(pieces, axis, split_axis=0, concat_axis=0, axis_index_grou...]
    all_to_all x1 -> x2, waiting for transfers between devices: 4.77 us -> 25.4 us  [exchange(): lax.all_to_all(pieces, axis, split_axis=0, concat_axis=0, axis_index_grou...]
    all_to_all x1 -> x2, starting transfers between devices: 6.6 us -> 20.5 us  [exchange(): lax.all_to_all(pieces, axis, split_axis=0, concat_axis=0, axis_index_grou...]
    all_gather x0 -> x2, blocking collectives: none -> 11.1 us  [paired(): lax.all_gather(part, 'narrow', axis_index_groups=members('narrow', 1, 2))]
    pallas_call x1 -> x3, Pallas kernels: 6.43 us -> 10 us  [the longest x1 6.42 us: factor(): pl.pallas_call(functools.partial(factor_kernel, root), out_shape=[square,...]
    unnamed x4 -> x3, local copies, waits for them, and re-layouts: 1.72 us -> 0.1 us
    dot_general x2 -> x0, matrix products: 1.24 us -> none  [product(): lax.dot_general(left, right, (dims, ((), ())), precision=lax.Precision.HI...]
    slice x1 -> x0, local copies, waits for them, and re-layouts: 1.2 us -> none  [factor(): return (inverse, upper, spread[0, 0])]
  transfers between devices with their start and end apart: 1 -> 2, of which waited for: 1 -> 2; matrix products, arithmetic and copies ran while one was open for 0% -> 0% of each run, Pallas kernels for 0% -> 0%
where the time goes in v3:
time: 89.6 us; the launch traced here: 89.2 us
  blocking collectives  30.9 us (34%)
  waiting for transfers between devices  25.4 us (28%)
  starting transfers between devices  20.5 us (23%)
  Pallas kernels  10 us (11%)
    all_to_all x2, waiting for transfers between devices, exchange(): lax.all_to_all(pieces, axis, split_axis=0, concat_axis=0, axis_index_grou...  25.4 us
    all_to_all x2, starting transfers between devices, exchange(): lax.all_to_all(pieces, axis, split_axis=0, concat_axis=0, axis_index_grou...  20.5 us
    all_to_all x2, blocking collectives, exchange(): lax.all_to_all(pieces, axis, split_axis=0, concat_axis=0, axis_index_grou...  19.9 us
    all_gather x2, blocking collectives, paired(): lax.all_gather(part, 'narrow', axis_index_groups=members('narrow', 1, 2))  11.1 us
    pallas_call x1, Pallas kernels, factor(): pl.pallas_call(functools.partial(factor_kernel, root), out_shape=[square,...  6.42 us
    pallas_call x1, Pallas kernels, apply(): pl.pallas_call(apply_kernel, out_shape=jax.ShapeDtypeStruct((length, orde...  2.32 us
  transfers between devices with their start and end apart: 2, of which 2 were waited for; matrix products, arithmetic and copies ran while one was open for 0% of the time, Pallas kernels for 0%

profile of v3, /device:TPU:1, one launch (start us, length us, event | category | flops | bytes accessed | tf_op | source)
XLA Modules:
  0.0 89.2 jit_solution(12344092967476000469)
XLA Ops:
  0.6 17.1 %all-to-all-start.3 = ((f32[512,2,128]{2,1,0:T(2,128)}), f32[512,2,128]{2,1,0:T(2,128)S(1)}, u32[]{:S(2)}, u32[]{:S(2)}) async-start(f32[512,2,128]{2,1,0:T(2,128)} %bitcast.44), calls=%async_computation.3 | async-start | bytes 1048576 | tf_op jit(solution)/shard_map/all_to_all | solution.py:30
  17.8 17.2 %all-to-all-done.3 = f32[512,2,128]{2,1,0:T(2,128)S(1)} async-done(((f32[512,2,128]{2,1,0:T(2,128)}), f32[512,2,128]{2,1,0:T(2,128)S(1)}, u32[]{:S(2)}, u32[]{:S(2)}) %all-to-all-start.3) | async-done | bytes 524320 | tf_op jit(solution)/shard_map/all_to_all | solution.py:30
  35.0 0.1 copy.11
  35.1 1.3 %gram.5 = f32[80,128]{1,0:T(8,128)} custom-call(f32[128,1024]{1,0:T(8,128)S(1)} %bitcast.39), custom_call_target="tpu_custom_call" | custom-call | tf_op jit(solution)/shard_map/gram/pallas_call | solution.py:80
  36.4 5.2 %all-gather.2 = f32[160,128]{1,0:T(8,128)S(1)} all-gather(f32[80,128]{1,0:T(8,128)} %gram.5), channel_id=4, replica_groups={{0,1},{2,3},{4,5},{6,7},{8,9},{10,11},{12,13},{14,15},{16,17},{18,19},{..., dimensions={0}, use_global_device_ids=true | all-gather | bytes 122880 | tf_op jit(solution)/shard_map/all_gather | solution.py:50
  41.7 8.4 %all_to_all.47 = f32[4,40,128]{2,1,0:T(8,128)S(1)} all-to-all(f32[4,40,128]{2,1,0:T(8,128)S(1)} %broadcast_in_dim.27), channel_id=1, replica_groups={{0,2,4,6},{1,3,5,7},{8,10,12,14},{9,11,13,15},{16,18,20,22},{17,19,21,2..., dimensions={0} | all-to-all | bytes 163840 | tf_op jit(solution)/shard_map/all_to_all | solution.py:30
  50.1 11.5 %all_to_all.48 = f32[8,40,128]{2,1,0:T(8,128)S(1)} all-to-all(f32[8,40,128]{2,1,0:T(8,128)S(1)} %broadcast_in_dim.28), channel_id=1, replica_groups={{0,8,16,24,32,40,48,56},{64,72,80,88,96,104,112,120},{128,136,144,152,1..., dimensions={0} | all-to-all | bytes 327680 | tf_op jit(solution)/shard_map/all_to_all | solution.py:30
  61.6 0.7 broadcast_in_dim.29
  62.3 3.4 %all-to-all-start.6 = ((f32[8,40,128]{2,1,0:T(8,128)}), f32[8,40,128]{2,1,0:T(8,128)S(1)}, u32[]{:S(2)}, u32[]{:S(2)}) async-start(f32[8,40,128]{2,1,0:T(8,128)} %broadcast_in_dim.29), calls=%async_computation.6 | async-start | bytes 327680 | tf_op jit(solution)/shard_map/all_to_all | solution.py:30
  65.7 8.2 %all-to-all-done.6 = f32[8,40,128]{2,1,0:T(8,128)S(1)} async-done(((f32[8,40,128]{2,1,0:T(8,128)}), f32[8,40,128]{2,1,0:T(8,128)S(1)}, u32[]{:S(2)}, u32[]{:S(2)}) %all-to-all-start.6) | async-done | bytes 163872 | tf_op jit(solution)/shard_map/all_to_all | solution.py:30
  73.9 5.9 %all-gather.3.packed_ref = f32[80,128]{1,0:T(8,128)} all-gather(f32[40,128]{1,0:T(8,128)S(1)} %reduce_sum.87), channel_id=5, replica_groups={{0,1},{2,3},{4,5},{6,7},{8,9},{10,11},{12,13},{14,15},{16,17},{18,19},{..., dimensions={0}, use_global_device_ids=true | all-gather | bytes 61440 | tf_op jit(solution)/shard_map/all_gather | solution.py:50
  79.8 6.4 %factor.5 = (f32[128,128]{1,0:T(8,128)S(1)}, f32[128,128]{1,0:T(8,128)S(1)}, f32[1,1]{1,0:T(1,128)}) custom-call(f32[80,128]{1,0:T(8,128)} %all-gather.3.packed_ref), custom_call_target="tpu_custom_call" | custom-call | tf_op jit(solution)/shard_map/factor/pallas_call | solution.py:170
  86.2 0.6 while.16
  86.8 0.0 copy-start.1
  86.8 2.3 %apply.1 = f32[1024,128]{1,0:T(8,128)} custom-call(f32[128,1024]{1,0:T(8,128)S(1)} %get-tuple-element.161, f32[128,128]{1,0:T(8,128)S(1)} %get-tuple-element.77.inverse_ref), custom_call_target="tpu_custom_call" | custom-call | tf_op jit(solution)/shard_map/apply/pallas_call | solution.py:188
  89.2 0.0 copy-done.1
  (9 shorter events, 0.1 us)
Async XLA Ops:
  0.6 34.3 %all-to-all-start.3 = ((f32[512,2,128]{2,1,0:T(2,128)}), f32[512,2,128]{2,1,0:T(2,128)S(1)}, u32[]{:S(2)}, u32[]{:S(2)}) async-start(f32[512,2,128]{2,1,0:T(2,128)} %bitcast.44), calls=%async_computation.3 | async-start | bytes 1048576 | tf_op jit(solution)/shard_map/all_to_all | solution.py:30
  62.3 11.6 %all-to-all-start.6 = ((f32[8,40,128]{2,1,0:T(8,128)}), f32[8,40,128]{2,1,0:T(8,128)S(1)}, u32[]{:S(2)}, u32[]{:S(2)}) async-start(f32[8,40,128]{2,1,0:T(8,128)} %broadcast_in_dim.29), calls=%async_computation.6 | async-start | bytes 327680 | tf_op jit(solution)/shard_map/all_to_all | solution.py:30
  86.8 2.3 %copy-start.1 = (f32[128,128]{1,0:T(8,128)}, f32[128,128]{1,0:T(8,128)S(1)}, u32[]{:S(2)}) copy-start(f32[128,128]{1,0:T(8,128)S(1)} %get-tuple-element.73) | copy-start | bytes 196612

commit v4 on v3

--- a/solution.py
+++ b/solution.py
@@ -3,6 +3,7 @@
 
 import jax
 import jax.numpy as jnp
+import numpy as np
 from jax import lax
 from jax.experimental import pallas as pl
 from jax.experimental.pallas import tpu as pltpu
@@ -32,58 +33,46 @@
     )
 
 
-def members(axis, stride, count):
-    size = lax.axis_size(axis)
-    return [
-        [first + step * stride for step in range(count)]
-        for block in range(0, size, stride * count)
-        for first in range(block, block + stride)
-    ]
-
-
-def added(part, axis, stride, count):
-    pieces = jnp.broadcast_to(part, (count, *part.shape))
-    return jnp.sum(exchange(pieces, axis, members(axis, stride, count)), axis=0)
-
-
-def paired(part):
-    return lax.all_gather(part, "narrow", axis_index_groups=members("narrow", 1, 2))
+EVERY = ("wide", "narrow")
+
+
+def added(part, groups):
+    pieces = jnp.broadcast_to(part, (len(groups[0]), *part.shape))
+    return jnp.sum(exchange(pieces, EVERY, groups), axis=0)
+
+
+def paired(part, groups):
+    return lax.all_gather(part, EVERY, axis_index_groups=groups)
 
 
 def total(packed):
+    wide, narrow = lax.axis_size("wide"), lax.axis_size("narrow")
+    side = math.isqrt(wide)
+    places = np.arange(wide * narrow).reshape(wide // side, side, narrow // 2, 2)
+    pairs = places.reshape(-1, 2).tolist()
+    spread = places.transpose(0, 1, 3, 2).reshape(-1, narrow // 2).tolist()
+    near = places.transpose(3, 2, 0, 1)
+    far = places.transpose(3, 2, 1, 0)
+    first = [near[0].reshape(-1, side), far[1].reshape(-1, wide // side)]
+    second = [far[0].reshape(-1, wide // side), near[1].reshape(-1, side)]
     half = packed.shape[0] // 2
-    both = jnp.sum(paired(packed), axis=0)
+    both = jnp.sum(paired(packed, pairs), axis=0)
     part = lax.dynamic_slice_in_dim(both, lax.axis_index("narrow") % 2 * half, half, axis=0)
-    side = math.isqrt(lax.axis_size("wide"))
-    part = added(part, "narrow", 2, lax.axis_size("narrow") // 2)
-    part = added(part, "wide", 1, side)
-    part = added(part, "wide", side, lax.axis_size("wide") // side)
-    return paired(part).reshape(packed.shape)
-
-
-def gram_kernel(columns_ref, packed_ref):
-    columns = columns_ref[...]
-    gram = product(columns, columns, ((1,), (1,)))
-    half = gram.shape[0] // 2
+    part = added(part, spread)
+    part = added(part, np.concatenate(first).tolist())
+    part = added(part, np.concatenate(second).tolist())
+    return paired(part, pairs).reshape(packed.shape)
+
+
+def gram(values, dim):
+    square = product(values, values, ((dim,), (dim,)))
+    half = square.shape[0] // 2
     across = lax.broadcasted_iota(jnp.int32, (half, 2 * half), 1)
     down = lax.broadcasted_iota(jnp.int32, (half, 2 * half), 0)
-    bottom = gram[half:, :]
-    packed_ref[:half, :] = jnp.where(across < down, pltpu.roll(bottom, half, 1), gram[:half, :])
+    bottom = square[half:, :]
+    rows = jnp.where(across < down, jnp.roll(bottom, half, axis=1), square[:half, :])
     corner = jnp.sum(jnp.where(across == down + half, bottom, 0.0), axis=0, keepdims=True)
-    rest = packed_ref.shape[0] - half
-    packed_ref[half:, :] = jnp.broadcast_to(corner, (rest, 2 * half))
-
-
-def gram(columns):
-    order = columns.shape[0]
-    rows = order // 2 + 2 * SUBLANES
-    return pl.pallas_call(
-        gram_kernel,
-        out_shape=jax.ShapeDtypeStruct((rows, order), jnp.float32),
-        in_specs=[pl.BlockSpec(memory_space=pltpu.VMEM)],
-        out_specs=pl.BlockSpec(memory_space=pltpu.VMEM),
-        name="gram",
-    )(columns)
+    return jnp.concatenate([rows, jnp.broadcast_to(corner, (2 * SUBLANES, 2 * half))], axis=0)
 
 
 def split(value):
@@ -109,7 +98,7 @@
     return jnp.concatenate(blocks, axis=0)
 
 
-def factor_kernel(root, packed_ref, inverse_ref, upper_ref, spread_ref, work):
+def factor_kernel(root, packed_ref, inverse_ref, upper_ref, status_ref, work):
     order = packed_ref.shape[1]
     half = order // 2
     across = lax.broadcasted_iota(jnp.int32, (order, order), 1)
@@ -158,44 +147,57 @@
             )
             work[end:, :] -= update[end:, :]
     inverse = jnp.where(across <= down, work[:, order:], 0.0)
-    spread_ref[...] = jnp.sum(inverse * inverse, keepdims=True)
+    place = lax.broadcasted_iota(jnp.int32, status_ref.shape, 1)
+    status_ref[...] = jnp.where(place == 0, jnp.sum(inverse * inverse, keepdims=True), 0.0)
     inverse_ref[...] = inverse * (scale * root)
     upper_ref[...] = jnp.where(across >= down, work[:, :order], 0.0) * (1.0 / (scale * root))
 
 
 def factor(packed, root):
     order = packed.shape[1]
-    square = jax.ShapeDtypeStruct((order, order), jnp.float32)
+    shape = jax.ShapeDtypeStruct((order, order), jnp.float32)
     whole = pl.BlockSpec(memory_space=pltpu.VMEM)
-    inverse, upper, spread = pl.pallas_call(
+    return pl.pallas_call(
         functools.partial(factor_kernel, root),
-        out_shape=[square, square, jax.ShapeDtypeStruct((1, 1), jnp.float32)],
+        out_shape=[shape, shape, jax.ShapeDtypeStruct((1, 2), jnp.float32)],
         in_specs=[whole],
         out_specs=[whole] * 3,
         scratch_shapes=[pltpu.VMEM((order, 2 * order), jnp.float32)],
         name="factor",
     )(packed)
-    return inverse, upper, spread.reshape(())
-
-
-def apply_kernel(columns_ref, inverse_ref, rows_ref):
-    rows_ref[...] = product(columns_ref[...], inverse_ref[...], ((0,), (1,)))
-
-
-def apply(columns, inverse):
-    order, length = columns.shape
-    step = math.gcd(length, 2 * LANES)
+
+
+def apply_kernel(tiles_ref, inverse_ref, rows_ref, buffer, done):
+    blocks = done.shape[0]
+    order = inverse_ref.shape[0]
+    copies = []
+    for block in range(blocks):
+        part = pl.ds(block * LANES, LANES)
+        values = tiles_ref[pl.ds(block, order, stride=blocks), :]
+        buffer[part, :] = product(values, inverse_ref[...], ((0,), (1,)))
+        copies.append(
+            pltpu.make_async_copy(buffer.at[part, :], rows_ref.at[part, :], done.at[block])
+        )
+        copies[-1].start()
+    for copy in copies:
+        copy.wait()
+
+
+def apply(tiles, inverse):
+    order = inverse.shape[0]
+    blocks = tiles.shape[0] // order
+    whole = pl.BlockSpec(memory_space=pltpu.VMEM)
     return pl.pallas_call(
         apply_kernel,
-        out_shape=jax.ShapeDtypeStruct((length, order), jnp.float32),
-        grid=(length // step,),
-        in_specs=[
-            pl.BlockSpec((order, step), lambda i: (0, i)),
-            pl.BlockSpec((order, order), lambda i: (0, 0)),
+        out_shape=jax.ShapeDtypeStruct((blocks * LANES, order), jnp.float32),
+        in_specs=[whole, whole],
+        out_specs=pl.BlockSpec(memory_space=pl.ANY),
+        scratch_shapes=[
+            pltpu.VMEM((blocks * LANES, order), jnp.float32),
+            pltpu.SemaphoreType.DMA((blocks,)),
         ],
-        out_specs=pl.BlockSpec((step, order), lambda i: (i, 0)),
         name="apply",
-    )(columns, inverse)
+    )(tiles, inverse)
 
 
 def shards(snapshots):
@@ -204,23 +206,25 @@
     tiles = length // LANES
     blocks = snapshots.reshape(held, tiles, LANES).transpose(1, 0, 2)
     blocks = exchange(blocks, "wide").reshape(groups, tiles // groups, held, LANES)
-    columns = blocks.transpose(0, 2, 1, 3).reshape(groups * held, length // groups)
+    tiles = blocks.transpose(0, 2, 1, 3).reshape(-1, LANES)
+    columns = tiles.reshape(groups * held, length // groups)
 
     root = math.sqrt(length * lax.axis_size("narrow"))
 
-    inverse, upper, spread = factor(total(gram(columns)), root)
+    inverse, upper, status = factor(total(gram(columns, 1)), root)
 
     def rough(state):
-        step, _, _, spread = state
-        return jnp.logical_and(step < PASSES, jnp.logical_not(spread <= LIMIT))
+        status = state[2]
+        return jnp.logical_and(status[0, 1] < PASSES - 1, jnp.logical_not(status[0, 0] <= LIMIT))
 
     def again(state):
-        step, inverse, upper, _ = state
-        more, next_upper, spread = factor(total(gram(product(inverse, columns))), root)
-        return step + 1, product(more, inverse), product(next_upper, upper), spread
-
-    _, inverse, upper, _ = lax.while_loop(rough, again, (jnp.int32(1), inverse, upper, spread))
-    return apply(columns, inverse), upper
+        inverse, upper, status = state
+        more, next_upper, fresh = factor(total(gram(apply(tiles, inverse), 0)), root)
+        status = jnp.concatenate([fresh[:, :1], status[:, 1:] + 1.0], axis=1)
+        return product(more, inverse), product(next_upper, upper), status
+
+    inverse, upper, _ = lax.while_loop(rough, again, (inverse, upper, status))
+    return apply(tiles, inverse), upper
 
 
 def solution(mesh):

time: 89.6 us -> 89.3 us (level)
  blocking collectives: 30.9 us -> 41.5 us
  waiting for transfers between devices: 25.4 us -> 17.1 us
  starting transfers between devices: 20.5 us -> 17.1 us
  Pallas kernels: 10 us -> 8.43 us
    all_to_all x2 -> x3, blocking collectives: 19.9 us -> 30.7 us  [exchange(): lax.all_to_all(pieces, axis, split_axis=0, concat_axis=0, axis_index_grou...]
    all_to_all x2 -> x1, waiting for transfers between devices: 25.4 us -> 17.1 us  [exchange(): lax.all_to_all(pieces, axis, split_axis=0, concat_axis=0, axis_index_grou...]
    all_to_all x2 -> x1, starting transfers between devices: 20.5 us -> 17.1 us  [exchange(): lax.all_to_all(pieces, axis, split_axis=0, concat_axis=0, axis_index_grou...]
    pallas_call x3 -> x2, Pallas kernels: 10 us -> 8.43 us  [the longest x1 6.46 us: factor(): pl.pallas_call(functools.partial(factor_kernel, root), out_shape=[shape,...]
    slice x0 -> x2, local copies, waits for them, and re-layouts: none -> 1.4 us  [the longest x1 1.32 us: rough(): status[0, 0] <= LIMIT]
  transfers between devices with their start and end apart: 2 -> 1, of which waited for: 2 -> 1; matrix products, arithmetic and copies ran while one was open for 0% -> 0% of each run, Pallas kernels for 0% -> 0%
where the time goes in v4:
time: 89.3 us; the launch traced here: 88.9 us
  blocking collectives  41.5 us (46%)
  starting transfers between devices  17.1 us (19%)
  waiting for transfers between devices  17.1 us (19%)
  Pallas kernels  8.43 us (9%)
  local copies, waits for them, and re-layouts  1.52 us (2%)
  loops' own time  1.48 us (2%)
  between operations  0.92 us (1%)
    all_to_all x3, blocking collectives, exchange(): lax.all_to_all(pieces, axis, split_axis=0, concat_axis=0, axis_index_grou...  30.7 us
    all_to_all x1, starting transfers between devices, exchange(): lax.all_to_all(pieces, axis, split_axis=0, concat_axis=0, axis_index_grou...  17.1 us
    all_to_all x1, waiting for transfers between devices, exchange(): lax.all_to_all(pieces, axis, split_axis=0, concat_axis=0, axis_index_grou...  17.1 us
    all_gather x2, blocking collectives, paired(): return lax.all_gather(part, EVERY, axis_index_groups=groups)  10.7 us
    pallas_call x1, Pallas kernels, factor(): pl.pallas_call(functools.partial(factor_kernel, root), out_shape=[shape,...  6.46 us
    pallas_call x1, Pallas kernels, apply(): pl.pallas_call(apply_kernel, out_shape=jax.ShapeDtypeStruct((blocks * LAN...  1.97 us
  transfers between devices with their start and end apart: 1, of which 1 were waited for; matrix products, arithmetic and copies ran while one was open for 0% of the time, Pallas kernels for 0%

profile of v4, /device:TPU:1, one launch (start us, length us, event | category | flops | bytes accessed | tf_op | source)
XLA Modules:
  0.0 88.9 jit_solution(12916452284405732838)
XLA Ops:
  0.6 17.1 %all-to-all-start.3 = ((f32[512,2,128]{2,1,0:T(2,128)}), f32[512,2,128]{2,1,0:T(2,128)S(1)}, u32[]{:S(2)}, u32[]{:S(2)}) async-start(f32[512,2,128]{2,1,0:T(2,128)} %bitcast.45), calls=%async_computation.3 | async-start | bytes 1048576 | tf_op jit(solution)/shard_map/all_to_all | solution.py:31
  17.8 17.1 %all-to-all-done.3 = f32[512,2,128]{2,1,0:T(2,128)S(1)} async-done(((f32[512,2,128]{2,1,0:T(2,128)}), f32[512,2,128]{2,1,0:T(2,128)S(1)}, u32[]{:S(2)}, u32[]{:S(2)}) %all-to-all-start.3) | async-done | bytes 524320 | tf_op jit(solution)/shard_map/all_to_all | solution.py:31
  35.0 0.6 fusion.1
  35.7 0.1 fusion.7
  35.8 0.1 slice_select_fusion.3
  35.9 5.0 %all-gather.2 = f32[160,128]{1,0:T(8,128)S(1)} all-gather(f32[80,128]{1,0:T(8,128)S(1)} %pad_maximum_fusion.2), channel_id=4, replica_groups={{0,1},{2,3},{4,5},{6,7},{8,9},{10,11},{12,13},{14,15},{16,17},{18,19},{..., dimensions={0}, use_global_device_ids=true | all-gather | bytes 122880 | tf_op jit(solution)/shard_map/all_gather | solution.py:45
  40.9 8.4 %all_to_all.47 = f32[4,40,128]{2,1,0:T(8,128)S(1)} all-to-all(f32[4,40,128]{2,1,0:T(8,128)S(1)} %broadcast_in_dim.55), channel_id=1, replica_groups={{0,2,4,6},{1,3,5,7},{8,10,12,14},{9,11,13,15},{16,18,20,22},{17,19,21,2..., dimensions={0} | all-to-all | bytes 163840 | tf_op jit(solution)/shard_map/all_to_all | solution.py:31
  49.3 11.3 %all_to_all.48 = f32[8,40,128]{2,1,0:T(8,128)S(1)} all-to-all(f32[8,40,128]{2,1,0:T(8,128)S(1)} %broadcast_in_dim.56), channel_id=1, replica_groups={{0,8,16,24,32,40,48,56},{64,72,80,88,96,104,112,120},{128,136,144,152,1..., dimensions={0} | all-to-all | bytes 327680 | tf_op jit(solution)/shard_map/all_to_all | solution.py:31
  60.7 11.1 %all_to_all.49 = f32[8,40,128]{2,1,0:T(8,128)S(1)} all-to-all(f32[8,40,128]{2,1,0:T(8,128)S(1)} %broadcast_in_dim.57), channel_id=1, replica_groups={{0,64,128,192,256,320,384,448},{8,72,136,200,264,328,392,456},{16,80,14..., dimensions={0} | all-to-all | bytes 327680 | tf_op jit(solution)/shard_map/all_to_all | solution.py:31
  71.8 5.7 %all-gather.3.packed_ref = f32[80,128]{1,0:T(8,128)} all-gather(f32[40,128]{1,0:T(8,128)S(1)} %reduce_sum.109), channel_id=5, replica_groups={{0,1},{2,3},{4,5},{6,7},{8,9},{10,11},{12,13},{14,15},{16,17},{18,19},{..., dimensions={0}, use_global_device_ids=true | all-gather | bytes 61440 | tf_op jit(solution)/shard_map/all_gather | solution.py:45
  77.5 6.5 %factor.5 = (f32[128,128]{1,0:T(8,128)S(1)}, f32[128,128]{1,0:T(8,128)S(1)}, f32[1,2]{1,0:T(1,128)}) custom-call(f32[80,128]{1,0:T(8,128)} %all-gather.3.packed_ref), custom_call_target="tpu_custom_call" | custom-call | tf_op jit(solution)/shard_map/factor/pallas_call | solution.py:160
  83.9 2.8 %while.14 = (f32[128,128]{1,0:T(8,128)S(1)}, f32[128,128]{1,0:T(8,128)S(1)}, f32[1,2]{1,0:T(1,128)}, f32[1024,128]{1,0:T(8,128)S(1)}, f32[]{:T(128)}, /*index=5*...) while((f32[128,128]{1,0:T(8,128)S(1)}, ...), condition=%wide.region_11.12_spmd, body=%wide.region_5.11_spmd.sunk | while | flops 251814848 | bytes 4331522 | solution.py:226
  83.9 1.3 %fusion.17 = (f32[1,1]{1,0:T(1,128)}, f32[1,1]{1,0:T(1,128)}) fusion(f32[1,2]{1,0:T(1,128)} %get-tuple-element.87), kind=kLoop, calls=%fused_computation.21.clone | loop fusion | bytes 16 | tf_op jit(solution)/shard_map/while/cond/slice | solution.py:218
  86.7 0.0 copy-start.2
  86.7 2.0 %apply.5 = f32[1024,128]{1,0:T(8,128)} custom-call(f32[1024,128]{1,0:T(8,128)S(1)} %get-tuple-element.160, f32[128,128]{1,0:T(8,128)S(1)} %get-tuple-element.63.inverse_ref), custom_call_target="tpu_custom_call" | custom-call | tf_op jit(solution)/shard_map/apply/pallas_call | solution.py:190
  88.7 0.0 copy-done.2
  (13 shorter events, 0.2 us)
Async XLA Ops:
  0.6 34.3 %all-to-all-start.3 = ((f32[512,2,128]{2,1,0:T(2,128)}), f32[512,2,128]{2,1,0:T(2,128)S(1)}, u32[]{:S(2)}, u32[]{:S(2)}) async-start(f32[512,2,128]{2,1,0:T(2,128)} %bitcast.45), calls=%async_computation.3 | async-start | bytes 1048576 | tf_op jit(solution)/shard_map/all_to_all | solution.py:31
  86.7 2.0 %copy-start.2 = (f32[128,128]{1,0:T(8,128)}, f32[128,128]{1,0:T(8,128)S(1)}, u32[]{:S(2)}) copy-start(f32[128,128]{1,0:T(8,128)S(1)} %get-tuple-element.59) | copy-start | bytes 196612

commit v5 on v4

--- a/solution.py
+++ b/solution.py
@@ -14,7 +14,9 @@
 PANEL = 16
 FLOOR = 1e-6
 LIMIT = 4096.0
-PASSES = 5
+CAP = 1e9
+GAIN = 64.0
+COPIES = 4
 
 
 def product(left, right, dims=((1,), (0,))):
@@ -48,19 +50,18 @@
 def total(packed):
     wide, narrow = lax.axis_size("wide"), lax.axis_size("narrow")
     side = math.isqrt(wide)
-    places = np.arange(wide * narrow).reshape(wide // side, side, narrow // 2, 2)
+    places = np.arange(wide * narrow).reshape(side // 2, 2, side // 2, 2, narrow // 2, 2)
     pairs = places.reshape(-1, 2).tolist()
-    spread = places.transpose(0, 1, 3, 2).reshape(-1, narrow // 2).tolist()
-    near = places.transpose(3, 2, 0, 1)
-    far = places.transpose(3, 2, 1, 0)
-    first = [near[0].reshape(-1, side), far[1].reshape(-1, wide // side)]
-    second = [far[0].reshape(-1, wide // side), near[1].reshape(-1, side)]
+    even, odd = places[..., 0], places[..., 1]
+    first = [even.transpose(0, 1, 3, 4, 2), odd.transpose(1, 2, 3, 4, 0)]
+    second = [even.transpose(2, 4, 3, 0, 1), odd.transpose(0, 4, 1, 2, 3)]
+    first = np.concatenate([part.reshape(-1, narrow // 2 * (side // 2)) for part in first])
+    second = np.concatenate([part.reshape(-1, 2 * side) for part in second])
     half = packed.shape[0] // 2
     both = jnp.sum(paired(packed, pairs), axis=0)
     part = lax.dynamic_slice_in_dim(both, lax.axis_index("narrow") % 2 * half, half, axis=0)
-    part = added(part, spread)
-    part = added(part, np.concatenate(first).tolist())
-    part = added(part, np.concatenate(second).tolist())
+    part = added(part, first.tolist())
+    part = added(part, second.tolist())
     return paired(part, pairs).reshape(packed.shape)
 
 
@@ -98,7 +99,7 @@
     return jnp.concatenate(blocks, axis=0)
 
 
-def factor_kernel(root, packed_ref, inverse_ref, upper_ref, status_ref, work):
+def factor_kernel(root, packed_ref, inverse_ref, upper_ref, spread_ref, work):
     order = packed_ref.shape[1]
     half = order // 2
     across = lax.broadcasted_iota(jnp.int32, (order, order), 1)
@@ -147,8 +148,7 @@
             )
             work[end:, :] -= update[end:, :]
     inverse = jnp.where(across <= down, work[:, order:], 0.0)
-    place = lax.broadcasted_iota(jnp.int32, status_ref.shape, 1)
-    status_ref[...] = jnp.where(place == 0, jnp.sum(inverse * inverse, keepdims=True), 0.0)
+    spread_ref[...] = jnp.minimum(jnp.sum(inverse * inverse, keepdims=True), CAP)
     inverse_ref[...] = inverse * (scale * root)
     upper_ref[...] = jnp.where(across >= down, work[:, :order], 0.0) * (1.0 / (scale * root))
 
@@ -157,28 +157,34 @@
     order = packed.shape[1]
     shape = jax.ShapeDtypeStruct((order, order), jnp.float32)
     whole = pl.BlockSpec(memory_space=pltpu.VMEM)
-    return pl.pallas_call(
+    inverse, upper, spread = pl.pallas_call(
         functools.partial(factor_kernel, root),
-        out_shape=[shape, shape, jax.ShapeDtypeStruct((1, 2), jnp.float32)],
+        out_shape=[shape, shape, jax.ShapeDtypeStruct((1, 1), jnp.float32)],
         in_specs=[whole],
         out_specs=[whole] * 3,
         scratch_shapes=[pltpu.VMEM((order, 2 * order), jnp.float32)],
         name="factor",
     )(packed)
+    return inverse, upper, spread.reshape(())
 
 
 def apply_kernel(tiles_ref, inverse_ref, rows_ref, buffer, done):
-    blocks = done.shape[0]
     order = inverse_ref.shape[0]
+    blocks = tiles_ref.shape[0] // order
+    group = blocks // done.shape[0]
     copies = []
     for block in range(blocks):
-        part = pl.ds(block * LANES, LANES)
         values = tiles_ref[pl.ds(block, order, stride=blocks), :]
-        buffer[part, :] = product(values, inverse_ref[...], ((0,), (1,)))
-        copies.append(
-            pltpu.make_async_copy(buffer.at[part, :], rows_ref.at[part, :], done.at[block])
-        )
-        copies[-1].start()
+        place = pl.ds(block * LANES, LANES)
+        buffer[place, :] = product(values, inverse_ref[...], ((0,), (1,)))
+        if block % group == group - 1:
+            part = pl.ds((block + 1 - group) * LANES, group * LANES)
+            copies.append(
+                pltpu.make_async_copy(
+                    buffer.at[part, :], rows_ref.at[part, :], done.at[block // group]
+                )
+            )
+            copies[-1].start()
     for copy in copies:
         copy.wait()
 
@@ -194,7 +200,7 @@
         out_specs=pl.BlockSpec(memory_space=pl.ANY),
         scratch_shapes=[
             pltpu.VMEM((blocks * LANES, order), jnp.float32),
-            pltpu.SemaphoreType.DMA((blocks,)),
+            pltpu.SemaphoreType.DMA((math.gcd(blocks, COPIES),)),
         ],
         name="apply",
     )(tiles, inverse)
@@ -211,19 +217,18 @@
 
     root = math.sqrt(length * lax.axis_size("narrow"))
 
-    inverse, upper, status = factor(total(gram(columns, 1)), root)
+    inverse, upper, spread = factor(total(gram(columns, 1)), root)
 
     def rough(state):
-        status = state[2]
-        return jnp.logical_and(status[0, 1] < PASSES - 1, jnp.logical_not(status[0, 0] <= LIMIT))
+        return state[2] > LIMIT
 
     def again(state):
-        inverse, upper, status = state
+        inverse, upper, spread = state
         more, next_upper, fresh = factor(total(gram(apply(tiles, inverse), 0)), root)
-        status = jnp.concatenate([fresh[:, :1], status[:, 1:] + 1.0], axis=1)
-        return product(more, inverse), product(next_upper, upper), status
-
-    inverse, upper, _ = lax.while_loop(rough, again, (inverse, upper, status))
+        fresh = jnp.minimum(fresh, spread / GAIN)
+        return product(more, inverse), product(next_upper, upper), fresh
+
+    inverse, upper, _ = lax.while_loop(rough, again, (inverse, upper, spread))
     return apply(tiles, inverse), upper
 
 

time: 89.3 us -> 83.1 us (0.931)
  blocking collectives: 41.5 us -> 37.4 us
  local copies, waits for them, and re-layouts: 1.52 us -> 0.21 us
    all_gather x2, blocking collectives: 10.7 us -> 7.44 us  [paired(): return lax.all_gather(part, EVERY, axis_index_groups=groups)]
    slice x1 -> x0, local copies, waits for them, and re-layouts: 1.32 us -> none  [rough(): status[0, 0] <= LIMIT]
    all_to_all x3 -> x2, blocking collectives: 30.7 us -> 30 us  [exchange(): lax.all_to_all(pieces, axis, split_axis=0, concat_axis=0, axis_index_grou...]
where the time goes in v5:
time: 83.1 us; the launch traced here: 82.8 us
  blocking collectives  37.4 us (45%)
  starting transfers between devices  17.1 us (21%)
  waiting for transfers between devices  17.1 us (21%)
  Pallas kernels  8.36 us (10%)
  between operations  0.9 us (1%)
    all_to_all x2, blocking collectives, exchange(): lax.all_to_all(pieces, axis, split_axis=0, concat_axis=0, axis_index_grou...  30 us
    all_to_all x1, starting transfers between devices, exchange(): lax.all_to_all(pieces, axis, split_axis=0, concat_axis=0, axis_index_grou...  17.1 us
    all_to_all x1, waiting for transfers between devices, exchange(): lax.all_to_all(pieces, axis, split_axis=0, concat_axis=0, axis_index_grou...  17.1 us
    all_gather x2, blocking collectives, paired(): return lax.all_gather(part, EVERY, axis_index_groups=groups)  7.44 us
    pallas_call x1, Pallas kernels, factor(): pl.pallas_call(functools.partial(factor_kernel, root), out_shape=[shape,...  6.42 us
    pallas_call x1, Pallas kernels, apply(): pl.pallas_call(apply_kernel, out_shape=jax.ShapeDtypeStruct((blocks * LAN...  1.94 us
  transfers between devices with their start and end apart: 1, of which 1 were waited for; matrix products, arithmetic and copies ran while one was open for 0% of the time, Pallas kernels for 0%

profile of v5, /device:TPU:1, one launch (start us, length us, event | category | flops | bytes accessed | tf_op | source)
XLA Modules:
  0.0 82.8 jit_solution(527537389548624306)
XLA Ops:
  0.6 17.1 %all-to-all-start.2 = ((f32[512,2,128]{2,1,0:T(2,128)}), f32[512,2,128]{2,1,0:T(2,128)S(1)}, u32[]{:S(2)}, u32[]{:S(2)}) async-start(f32[512,2,128]{2,1,0:T(2,128)} %bitcast.44), calls=%async_computation.2 | async-start | bytes 1048576 | tf_op jit(solution)/shard_map/all_to_all | solution.py:33
  17.8 17.1 %all-to-all-done.2 = f32[512,2,128]{2,1,0:T(2,128)S(1)} async-done(((f32[512,2,128]{2,1,0:T(2,128)}), f32[512,2,128]{2,1,0:T(2,128)S(1)}, u32[]{:S(2)}, u32[]{:S(2)}) %all-to-all-start.2) | async-done | bytes 524320 | tf_op jit(solution)/shard_map/all_to_all | solution.py:33
  35.0 0.6 fusion.1
  35.7 0.1 fusion.6
  35.8 0.1 slice_select_fusion.3
  35.9 5.0 %all-gather.2 = f32[160,128]{1,0:T(8,128)S(1)} all-gather(f32[80,128]{1,0:T(8,128)S(1)} %pad_maximum_fusion.1), channel_id=4, replica_groups={{0,1},{2,3},{4,5},{6,7},{8,9},{10,11},{12,13},{14,15},{16,17},{18,19},{..., dimensions={0}, use_global_device_ids=true | all-gather | bytes 122880 | tf_op jit(solution)/shard_map/all_gather | solution.py:47
  40.9 16.7 %all_to_all.33 = f32[16,40,128]{2,1,0:T(8,128)S(1)} all-to-all(f32[16,40,128]{2,1,0:T(8,128)S(1)} %broadcast_in_dim.46), channel_id=1, replica_groups={{0,16,32,48,2,18,34,50,4,20,36,52,6,22,38,54},{8,24,40,56,10,26,42,58,1..., dimensions={0} | all-to-all | bytes 655360 | tf_op jit(solution)/shard_map/all_to_all | solution.py:33
  57.7 13.3 %all_to_all.34 = f32[16,40,128]{2,1,0:T(8,128)S(1)} all-to-all(f32[16,40,128]{2,1,0:T(8,128)S(1)} %broadcast_in_dim.47), channel_id=1, replica_groups={{0,64,128,192,256,320,384,448,8,72,136,200,264,328,392,456},{2,66,130,1..., dimensions={0} | all-to-all | bytes 655360 | tf_op jit(solution)/shard_map/all_to_all | solution.py:33
  71.0 2.4 %all-gather.3.packed_ref = f32[80,128]{1,0:T(8,128)} all-gather(f32[40,128]{1,0:T(8,128)S(1)} %reduce_sum.87), channel_id=5, replica_groups={{0,1},{2,3},{4,5},{6,7},{8,9},{10,11},{12,13},{14,15},{16,17},{18,19},{..., dimensions={0}, use_global_device_ids=true | all-gather | bytes 61440 | tf_op jit(solution)/shard_map/all_gather | solution.py:47
  73.4 6.4 %factor.5 = (f32[128,128]{1,0:T(8,128)S(1)}, f32[128,128]{1,0:T(8,128)S(1)}, f32[1,1]{1,0:T(1,128)}) custom-call(f32[80,128]{1,0:T(8,128)} %all-gather.3.packed_ref), custom_call_target="tpu_custom_call" | custom-call | tf_op jit(solution)/shard_map/factor/pallas_call | solution.py:160
  79.8 0.8 while.14
  80.6 0.0 copy-start.2
  80.7 1.9 %apply.5 = f32[1024,128]{1,0:T(8,128)} custom-call(f32[1024,128]{1,0:T(8,128)S(1)} %get-tuple-element.156, f32[128,128]{1,0:T(8,128)S(1)} %get-tuple-element.63.inverse_ref), custom_call_target="tpu_custom_call" | custom-call | tf_op jit(solution)/shard_map/apply/pallas_call | solution.py:196
  82.6 0.0 copy-done.2
  (11 shorter events, 0.2 us)
Async XLA Ops:
  0.6 34.3 %all-to-all-start.2 = ((f32[512,2,128]{2,1,0:T(2,128)}), f32[512,2,128]{2,1,0:T(2,128)S(1)}, u32[]{:S(2)}, u32[]{:S(2)}) async-start(f32[512,2,128]{2,1,0:T(2,128)} %bitcast.44), calls=%async_computation.2 | async-start | bytes 1048576 | tf_op jit(solution)/shard_map/all_to_all | solution.py:33
  80.6 2.0 %copy-start.2 = (f32[128,128]{1,0:T(8,128)}, f32[128,128]{1,0:T(8,128)S(1)}, u32[]{:S(2)}) copy-start(f32[128,128]{1,0:T(8,128)S(1)} %get-tuple-element.59) | copy-start | bytes 196612

commit v6 on v5

--- a/solution.py
+++ b/solution.py
@@ -16,7 +16,6 @@
 LIMIT = 4096.0
 CAP = 1e9
 GAIN = 64.0
-COPIES = 4
 
 
 def product(left, right, dims=((1,), (0,))):
@@ -82,6 +81,10 @@
     middle = rest.astype(jnp.bfloat16)
     low = (rest - middle.astype(jnp.float32)).astype(jnp.bfloat16)
     return high, middle, low
+
+
+def bf16_product(left, right):
+    return jnp.dot(left, right, preferred_element_type=jnp.float32)
 
 
 def replicated(value):
@@ -170,21 +173,23 @@
 
 def apply_kernel(tiles_ref, inverse_ref, rows_ref, buffer, done):
     order = inverse_ref.shape[0]
-    blocks = tiles_ref.shape[0] // order
-    group = blocks // done.shape[0]
+    blocks = done.shape[0]
+    high, middle, low = split(jnp.transpose(inverse_ref[...]))
+    double = jnp.concatenate([high, middle], axis=1)
+    double = jnp.concatenate([double, double], axis=0)
+    single = jnp.concatenate([low, high], axis=0)
     copies = []
     for block in range(blocks):
-        values = tiles_ref[pl.ds(block, order, stride=blocks), :]
-        place = pl.ds(block * LANES, LANES)
-        buffer[place, :] = product(values, inverse_ref[...], ((0,), (1,)))
-        if block % group == group - 1:
-            part = pl.ds((block + 1 - group) * LANES, group * LANES)
-            copies.append(
-                pltpu.make_async_copy(
-                    buffer.at[part, :], rows_ref.at[part, :], done.at[block // group]
-                )
-            )
-            copies[-1].start()
+        values = jnp.transpose(tiles_ref[pl.ds(block, order, stride=blocks), :])
+        high, middle, low = split(values)
+        most = bf16_product(jnp.concatenate([high, middle], axis=1), double)
+        rest = bf16_product(jnp.concatenate([high, low], axis=1), single)
+        part = pl.ds(block * LANES, LANES)
+        buffer[part, :] = most[:, :order] + (most[:, order:] + rest)
+        copies.append(
+            pltpu.make_async_copy(buffer.at[part, :], rows_ref.at[part, :], done.at[block])
+        )
+        copies[-1].start()
     for copy in copies:
         copy.wait()
 
@@ -200,7 +205,7 @@
         out_specs=pl.BlockSpec(memory_space=pl.ANY),
         scratch_shapes=[
             pltpu.VMEM((blocks * LANES, order), jnp.float32),
-            pltpu.SemaphoreType.DMA((math.gcd(blocks, COPIES),)),
+            pltpu.SemaphoreType.DMA((blocks,)),
         ],
         name="apply",
     )(tiles, inverse)

time: 83.1 us -> 82.4 us (level)
  no operation moved by 1% of the time
where the time goes in v6:
time: 82.4 us; the launch traced here: 82 us
  blocking collectives  37.4 us (45%)
  starting transfers between devices  17.1 us (21%)
  waiting for transfers between devices  17.1 us (21%)
  Pallas kernels  7.64 us (9%)
  between operations  0.9 us (1%)
    all_to_all x2, blocking collectives, exchange(): lax.all_to_all(pieces, axis, split_axis=0, concat_axis=0, axis_index_grou...  30 us
    all_to_all x1, starting transfers between devices, exchange(): lax.all_to_all(pieces, axis, split_axis=0, concat_axis=0, axis_index_grou...  17.1 us
    all_to_all x1, waiting for transfers between devices, exchange(): lax.all_to_all(pieces, axis, split_axis=0, concat_axis=0, axis_index_grou...  17.1 us
    all_gather x2, blocking collectives, paired(): return lax.all_gather(part, EVERY, axis_index_groups=groups)  7.44 us
    pallas_call x1, Pallas kernels, factor(): pl.pallas_call(functools.partial(factor_kernel, root), out_shape=[shape,...  6.42 us
  transfers between devices with their start and end apart: 1, of which 1 were waited for; matrix products, arithmetic and copies ran while one was open for 0% of the time, Pallas kernels for 0%

profile of v6, /device:TPU:1, one launch (start us, length us, event | category | flops | bytes accessed | tf_op | source)
XLA Modules:
  0.0 82.0 jit_solution(15602169264285087721)
XLA Ops:
  0.6 17.1 %all-to-all-start.2 = ((f32[512,2,128]{2,1,0:T(2,128)}), f32[512,2,128]{2,1,0:T(2,128)S(1)}, u32[]{:S(2)}, u32[]{:S(2)}) async-start(f32[512,2,128]{2,1,0:T(2,128)} %bitcast.44), calls=%async_computation.2 | async-start | bytes 1048576 | tf_op jit(solution)/shard_map/all_to_all | solution.py:32
  17.8 17.1 %all-to-all-done.2 = f32[512,2,128]{2,1,0:T(2,128)S(1)} async-done(((f32[512,2,128]{2,1,0:T(2,128)}), f32[512,2,128]{2,1,0:T(2,128)S(1)}, u32[]{:S(2)}, u32[]{:S(2)}) %all-to-all-start.2) | async-done | bytes 524320 | tf_op jit(solution)/shard_map/all_to_all | solution.py:32
  35.0 0.6 fusion.1
  35.7 0.1 fusion.6
  35.8 0.1 slice_select_fusion.3
  35.9 5.0 %all-gather.2 = f32[160,128]{1,0:T(8,128)S(1)} all-gather(f32[80,128]{1,0:T(8,128)S(1)} %pad_maximum_fusion.1), channel_id=4, replica_groups={{0,1},{2,3},{4,5},{6,7},{8,9},{10,11},{12,13},{14,15},{16,17},{18,19},{..., dimensions={0}, use_global_device_ids=true | all-gather | bytes 122880 | tf_op jit(solution)/shard_map/all_gather | solution.py:46
  40.9 16.7 %all_to_all.33 = f32[16,40,128]{2,1,0:T(8,128)S(1)} all-to-all(f32[16,40,128]{2,1,0:T(8,128)S(1)} %broadcast_in_dim.46), channel_id=1, replica_groups={{0,16,32,48,2,18,34,50,4,20,36,52,6,22,38,54},{8,24,40,56,10,26,42,58,1..., dimensions={0} | all-to-all | bytes 655360 | tf_op jit(solution)/shard_map/all_to_all | solution.py:32
  57.7 13.3 %all_to_all.34 = f32[16,40,128]{2,1,0:T(8,128)S(1)} all-to-all(f32[16,40,128]{2,1,0:T(8,128)S(1)} %broadcast_in_dim.47), channel_id=1, replica_groups={{0,64,128,192,256,320,384,448,8,72,136,200,264,328,392,456},{2,66,130,1..., dimensions={0} | all-to-all | bytes 655360 | tf_op jit(solution)/shard_map/all_to_all | solution.py:32
  71.0 2.4 %all-gather.3.packed_ref = f32[80,128]{1,0:T(8,128)} all-gather(f32[40,128]{1,0:T(8,128)S(1)} %reduce_sum.87), channel_id=5, replica_groups={{0,1},{2,3},{4,5},{6,7},{8,9},{10,11},{12,13},{14,15},{16,17},{18,19},{..., dimensions={0}, use_global_device_ids=true | all-gather | bytes 61440 | tf_op jit(solution)/shard_map/all_gather | solution.py:46
  73.4 6.4 %factor.5 = (f32[128,128]{1,0:T(8,128)S(1)}, f32[128,128]{1,0:T(8,128)S(1)}, f32[1,1]{1,0:T(1,128)}) custom-call(f32[80,128]{1,0:T(8,128)} %all-gather.3.packed_ref), custom_call_target="tpu_custom_call" | custom-call | tf_op jit(solution)/shard_map/factor/pallas_call | solution.py:163
  79.8 0.8 while.14
  80.6 0.0 copy-start.2
  80.7 1.2 %apply.5 = f32[1024,128]{1,0:T(8,128)} custom-call(f32[1024,128]{1,0:T(8,128)S(1)} %get-tuple-element.156, f32[128,128]{1,0:T(8,128)S(1)} %get-tuple-element.63.inverse_ref), custom_call_target="tpu_custom_call" | custom-call | tf_op jit(solution)/shard_map/apply/pallas_call | solution.py:201
  81.9 0.0 copy-done.2
  (11 shorter events, 0.2 us)
Async XLA Ops:
  0.6 34.3 %all-to-all-start.2 = ((f32[512,2,128]{2,1,0:T(2,128)}), f32[512,2,128]{2,1,0:T(2,128)S(1)}, u32[]{:S(2)}, u32[]{:S(2)}) async-start(f32[512,2,128]{2,1,0:T(2,128)} %bitcast.44), calls=%async_computation.2 | async-start | bytes 1048576 | tf_op jit(solution)/shard_map/all_to_all | solution.py:32
  80.6 1.2 %copy-start.2 = (f32[128,128]{1,0:T(8,128)}, f32[128,128]{1,0:T(8,128)S(1)}, u32[]{:S(2)}) copy-start(f32[128,128]{1,0:T(8,128)S(1)} %get-tuple-element.59) | copy-start | bytes 196612

commit v7 on v6

--- a/solution.py
+++ b/solution.py
@@ -59,9 +59,10 @@
     half = packed.shape[0] // 2
     both = jnp.sum(paired(packed, pairs), axis=0)
     part = lax.dynamic_slice_in_dim(both, lax.axis_index("narrow") % 2 * half, half, axis=0)
+    part = part.reshape(1, -1)
     part = added(part, first.tolist())
     part = added(part, second.tolist())
-    return paired(part, pairs).reshape(packed.shape)
+    return paired(part.reshape(half, -1), pairs)
 
 
 def gram(values, dim):
@@ -72,7 +73,7 @@
     bottom = square[half:, :]
     rows = jnp.where(across < down, jnp.roll(bottom, half, axis=1), square[:half, :])
     corner = jnp.sum(jnp.where(across == down + half, bottom, 0.0), axis=0, keepdims=True)
-    return jnp.concatenate([rows, jnp.broadcast_to(corner, (2 * SUBLANES, 2 * half))], axis=0)
+    return jnp.concatenate([rows, jnp.broadcast_to(corner, (2, 2 * half))], axis=0)
 
 
 def split(value):
@@ -103,13 +104,15 @@
 
 
 def factor_kernel(root, packed_ref, inverse_ref, upper_ref, spread_ref, work):
-    order = packed_ref.shape[1]
+    order = packed_ref.shape[2]
     half = order // 2
+    rows = packed_ref.shape[1]
     across = lax.broadcasted_iota(jnp.int32, (order, order), 1)
     down = lax.broadcasted_iota(jnp.int32, (order, order), 0)
-    top = packed_ref[:half, :]
+    top = jnp.concatenate([packed_ref[0], packed_ref[1, : half - rows]], axis=0)
+    corner = packed_ref[1, half - rows : half - rows + 1]
     flipped = pltpu.roll(jnp.transpose(jnp.concatenate([top, top], axis=0))[:half, :], half, 1)
-    bottom = jnp.where((across == down + half)[:half, :], packed_ref[half : half + 1, :], flipped)
+    bottom = jnp.where((across == down + half)[:half, :], corner, flipped)
     gram = jnp.concatenate([top, bottom], axis=0)
     diagonal = jnp.where(across == down, gram, 0.0)
     scale = lax.rsqrt(jnp.sum(diagonal, axis=0, keepdims=True))
@@ -117,10 +120,11 @@
     work[:, order:] = jnp.where(across == down, 1.0, 0.0)
     for base in range(0, order, PANEL):
         end = base + PANEL
-        panel = work[base:end, base:end]
+        panel = work[base:end, :order]
         entry = {}
         for col in range(PANEL):
-            spread_col = jnp.broadcast_to(panel[:, col : col + 1], (PANEL, LANES))
+            lanes = jnp.full(panel.shape, base + col, jnp.int32)
+            spread_col = jnp.take_along_axis(panel, lanes, axis=1)
             for row in range(col + 1):
                 entry[row, col] = replicated(spread_col[row : row + 1, :])
         left = [replicated(work[base + row : base + row + 1, :order]) for row in range(PANEL)]
@@ -157,7 +161,7 @@
 
 
 def factor(packed, root):
-    order = packed.shape[1]
+    order = packed.shape[2]
     shape = jax.ShapeDtypeStruct((order, order), jnp.float32)
     whole = pl.BlockSpec(memory_space=pltpu.VMEM)
     inverse, upper, spread = pl.pallas_call(

time: 82.4 us -> 81.8 us (level)
    all_to_all x2, blocking collectives: 30 us -> 28.9 us  [exchange(): lax.all_to_all(pieces, axis, split_axis=0, concat_axis=0, axis_index_grou...]
where the time goes in v7:
time: 81.8 us; the launch traced here: 81.5 us
  blocking collectives  36.7 us (45%)
  starting transfers between devices  17.1 us (21%)
  waiting for transfers between devices  17.1 us (21%)
  Pallas kernels  7.26 us (9%)
  between operations  0.91 us (1%)
  loops' own time  0.82 us (1%)
    all_to_all x2, blocking collectives, exchange(): lax.all_to_all(pieces, axis, split_axis=0, concat_axis=0, axis_index_grou...  28.9 us
    all_to_all x1, starting transfers between devices, exchange(): lax.all_to_all(pieces, axis, split_axis=0, concat_axis=0, axis_index_grou...  17.1 us
    all_to_all x1, waiting for transfers between devices, exchange(): lax.all_to_all(pieces, axis, split_axis=0, concat_axis=0, axis_index_grou...  17.1 us
    all_gather x2, blocking collectives, paired(): return lax.all_gather(part, EVERY, axis_index_groups=groups)  7.8 us
    pallas_call x1, Pallas kernels, factor(): pl.pallas_call(functools.partial(factor_kernel, root), out_shape=[shape,...  6.04 us
  transfers between devices with their start and end apart: 1, of which 1 were waited for; matrix products, arithmetic and copies ran while one was open for 0% of the time, Pallas kernels for 0%

profile of v7, /device:TPU:1, one launch (start us, length us, event | category | flops | bytes accessed | tf_op | source)
XLA Modules:
  0.0 81.5 jit_solution(2277347686121370266)
XLA Ops:
  0.6 17.1 %all-to-all-start.2 = ((f32[512,2,128]{2,1,0:T(2,128)}), f32[512,2,128]{2,1,0:T(2,128)S(1)}, u32[]{:S(2)}, u32[]{:S(2)}) async-start(f32[512,2,128]{2,1,0:T(2,128)} %bitcast.56), calls=%async_computation.2 | async-start | bytes 1048576 | tf_op jit(solution)/shard_map/all_to_all | solution.py:32
  17.8 17.1 %all-to-all-done.2 = f32[512,2,128]{2,1,0:T(2,128)S(1)} async-done(((f32[512,2,128]{2,1,0:T(2,128)}), f32[512,2,128]{2,1,0:T(2,128)S(1)}, u32[]{:S(2)}, u32[]{:S(2)}) %all-to-all-start.2) | async-done | bytes 524320 | tf_op jit(solution)/shard_map/all_to_all | solution.py:32
  35.0 0.6 fusion.1
  35.7 0.1 fusion.6
  35.8 0.1 slice_select_fusion.3
  35.9 5.0 %all-gather.3 = f32[2,66,128]{2,1,0:T(8,128)S(1)} all-gather(f32[1,66,128]{2,1,0:T(8,128)S(1)} %maximum_bitcast_fusion.1), channel_id=3, replica_groups={{0,1},{2,3},{4,5},{6,7},{8,9},{10,11},{12,13},{14,15},{16,17},{18,19},{..., dimensions={0}, use_global_device_ids=true | all-gather | bytes 101376 | tf_op jit(solution)/shard_map/all_gather | solution.py:46
  40.9 0.1 broadcast_in_dim.46
  41.1 16.1 %all_to_all.33 = f32[16,1,4224]{2,1,0:T(1,128)S(1)} all-to-all(f32[16,1,4224]{2,1,0:T(1,128)S(1)} %broadcast_in_dim.46), channel_id=1, replica_groups={{0,16,32,48,2,18,34,50,4,20,36,52,6,22,38,54},{8,24,40,56,10,26,42,58,1..., dimensions={0} | all-to-all | bytes 540672 | tf_op jit(solution)/shard_map/all_to_all | solution.py:32
  57.2 0.2 reduce_sum.80
  57.3 0.1 broadcast_in_dim.47
  57.5 12.8 %all_to_all.34 = f32[16,1,4224]{2,1,0:T(1,128)S(1)} all-to-all(f32[16,1,4224]{2,1,0:T(1,128)S(1)} %broadcast_in_dim.47), channel_id=1, replica_groups={{0,64,128,192,256,320,384,448,8,72,136,200,264,328,392,456},{2,66,130,1..., dimensions={0} | all-to-all | bytes 540672 | tf_op jit(solution)/shard_map/all_to_all | solution.py:32
  70.3 0.2 reduce_sum.81
  70.4 2.8 %all_gather.26.packed_ref = f32[2,33,128]{2,1,0:T(8,128)} all-gather(f32[1,33,128]{2,1,0:T(8,128)S(1)} %bitcast.57), channel_id=1, replica_groups={{0,1},{2,3},{4,5},{6,7},{8,9},{10,11},{12,13},{14,15},{16,17},{18,19},{..., dimensions={0}, use_global_device_ids=true | all-gather | bytes 50688 | tf_op jit(solution)/shard_map/all_gather | solution.py:46
  73.2 6.0 %factor.5 = (f32[128,128]{1,0:T(8,128)S(1)}, f32[128,128]{1,0:T(8,128)S(1)}, f32[1,1]{1,0:T(1,128)}) custom-call(f32[2,33,128]{2,1,0:T(8,128)} %all_gather.26.packed_ref), custom_call_target="tpu_custom_call" | custom-call | tf_op jit(solution)/shard_map/factor/pallas_call | solution.py:167
  79.3 0.8 %while.14 = (f32[128,128]{1,0:T(8,128)S(1)}, f32[128,128]{1,0:T(8,128)S(1)}, f32[]{:T(128)}, f32[1024,128]{1,0:T(8,128)S(1)}, f32[]{:T(128)}, /*index=5*/u32[]{:...) while((f32[128,128]{1,0:T(8,128)S(1)}, f32[128,128]{1,0:T(8,128)S(1)}, ...), condition=%wide.region_9.10_spmd, body=%wide.region_4.9_spmd.sunk | while | flops 251850944 | bytes 4824472 | solution.py:240
  80.1 0.0 copy-start.2
  80.1 1.2 %apply.5 = f32[1024,128]{1,0:T(8,128)} custom-call(f32[1024,128]{1,0:T(8,128)S(1)} %get-tuple-element.156, f32[128,128]{1,0:T(8,128)S(1)} %get-tuple-element.63.inverse_ref), custom_call_target="tpu_custom_call" | custom-call | tf_op jit(solution)/shard_map/apply/pallas_call | solution.py:205
  81.3 0.0 copy-done.2
  (7 shorter events, 0.1 us)
Async XLA Ops:
  0.6 34.3 %all-to-all-start.2 = ((f32[512,2,128]{2,1,0:T(2,128)}), f32[512,2,128]{2,1,0:T(2,128)S(1)}, u32[]{:S(2)}, u32[]{:S(2)}) async-start(f32[512,2,128]{2,1,0:T(2,128)} %bitcast.56), calls=%async_computation.2 | async-start | bytes 1048576 | tf_op jit(solution)/shard_map/all_to_all | solution.py:32
  80.1 1.2 %copy-start.2 = (f32[128,128]{1,0:T(8,128)}, f32[128,128]{1,0:T(8,128)S(1)}, u32[]{:S(2)}) copy-start(f32[128,128]{1,0:T(8,128)S(1)} %get-tuple-element.59) | copy-start | bytes 196612

commit v8 on v7

--- a/solution.py
+++ b/solution.py
@@ -51,11 +51,8 @@
     side = math.isqrt(wide)
     places = np.arange(wide * narrow).reshape(side // 2, 2, side // 2, 2, narrow // 2, 2)
     pairs = places.reshape(-1, 2).tolist()
-    even, odd = places[..., 0], places[..., 1]
-    first = [even.transpose(0, 1, 3, 4, 2), odd.transpose(1, 2, 3, 4, 0)]
-    second = [even.transpose(2, 4, 3, 0, 1), odd.transpose(0, 4, 1, 2, 3)]
-    first = np.concatenate([part.reshape(-1, narrow // 2 * (side // 2)) for part in first])
-    second = np.concatenate([part.reshape(-1, 2 * side) for part in second])
+    first = places.transpose(5, 0, 1, 3, 4, 2).reshape(-1, narrow // 2 * (side // 2))
+    second = places.transpose(5, 2, 4, 3, 0, 1).reshape(-1, 2 * side)
     half = packed.shape[0] // 2
     both = jnp.sum(paired(packed, pairs), axis=0)
     part = lax.dynamic_slice_in_dim(both, lax.axis_index("narrow") % 2 * half, half, axis=0)
@@ -170,6 +167,7 @@
         in_specs=[whole],
         out_specs=[whole] * 3,
         scratch_shapes=[pltpu.VMEM((order, 2 * order), jnp.float32)],
+        compiler_params=pltpu.CompilerParams(vmem_limit_bytes=8 * 1024 * 1024),
         name="factor",
     )(packed)
     return inverse, upper, spread.reshape(())
@@ -211,6 +209,7 @@
             pltpu.VMEM((blocks * LANES, order), jnp.float32),
             pltpu.SemaphoreType.DMA((blocks,)),
         ],
+        compiler_params=pltpu.CompilerParams(vmem_limit_bytes=8 * 1024 * 1024),
         name="apply",
     )(tiles, inverse)
 

time: 81.8 us -> 83.6 us (1.022)
  blocking collectives: 36.7 us -> 39.4 us
  Pallas kernels: 7.26 us -> 6.42 us
    all_gather x2, blocking collectives: 7.8 us -> 10 us  [paired(): return lax.all_gather(part, EVERY, axis_index_groups=groups)]
    pallas_call x1, Pallas kernels: 6.04 us -> 5.2 us  [factor(): pl.pallas_call(functools.partial(factor_kernel, root), out_shape=[shape,...]
where the time goes in v8:
time: 83.6 us; the launch traced here: 83.3 us
  blocking collectives  39.4 us (47%)
  starting transfers between devices  17.1 us (20%)
  waiting for transfers between devices  17.1 us (20%)
  Pallas kernels  6.42 us (8%)
  between operations  0.91 us (1%)
    all_to_all x2, blocking collectives, exchange(): lax.all_to_all(pieces, axis, split_axis=0, concat_axis=0, axis_index_grou...  29.3 us
    all_to_all x1, starting transfers between devices, exchange(): lax.all_to_all(pieces, axis, split_axis=0, concat_axis=0, axis_index_grou...  17.1 us
    all_to_all x1, waiting for transfers between devices, exchange(): lax.all_to_all(pieces, axis, split_axis=0, concat_axis=0, axis_index_grou...  17.1 us
    all_gather x2, blocking collectives, paired(): return lax.all_gather(part, EVERY, axis_index_groups=groups)  10 us
    pallas_call x1, Pallas kernels, factor(): pl.pallas_call(functools.partial(factor_kernel, root), out_shape=[shape,...  5.2 us
  transfers between devices with their start and end apart: 1, of which 1 were waited for; matrix products, arithmetic and copies ran while one was open for 0% of the time, Pallas kernels for 0%

profile of v8, /device:TPU:1, one launch (start us, length us, event | category | flops | bytes accessed | tf_op | source)
XLA Modules:
  0.0 83.3 jit_solution(9724083756684748042)
XLA Ops:
  0.6 17.1 %all-to-all-start.2 = ((f32[512,2,128]{2,1,0:T(2,128)}), f32[512,2,128]{2,1,0:T(2,128)S(1)}, u32[]{:S(2)}, u32[]{:S(2)}) async-start(f32[512,2,128]{2,1,0:T(2,128)} %bitcast.56), calls=%async_computation.2 | async-start | bytes 1048576 | tf_op jit(solution)/shard_map/all_to_all | solution.py:32
  17.8 17.1 %all-to-all-done.2 = f32[512,2,128]{2,1,0:T(2,128)S(1)} async-done(((f32[512,2,128]{2,1,0:T(2,128)}), f32[512,2,128]{2,1,0:T(2,128)S(1)}, u32[]{:S(2)}, u32[]{:S(2)}) %all-to-all-start.2) | async-done | bytes 524320 | tf_op jit(solution)/shard_map/all_to_all | solution.py:32
  35.0 0.6 fusion.1
  35.7 0.1 fusion.6
  35.8 0.1 slice_select_fusion.3
  35.9 5.0 %all-gather.3 = f32[2,66,128]{2,1,0:T(8,128)S(1)} all-gather(f32[1,66,128]{2,1,0:T(8,128)S(1)} %maximum_bitcast_fusion.1), channel_id=3, replica_groups={{0,1},{2,3},{4,5},{6,7},{8,9},{10,11},{12,13},{14,15},{16,17},{18,19},{..., dimensions={0}, use_global_device_ids=true | all-gather | bytes 101376 | tf_op jit(solution)/shard_map/all_gather | solution.py:46
  40.9 0.1 broadcast_in_dim.46
  41.1 18.5 %all_to_all.33 = f32[16,1,4224]{2,1,0:T(1,128)S(1)} all-to-all(f32[16,1,4224]{2,1,0:T(1,128)S(1)} %broadcast_in_dim.46), channel_id=1, replica_groups={{0,16,32,48,2,18,34,50,4,20,36,52,6,22,38,54},{8,24,40,56,10,26,42,58,1..., dimensions={0} | all-to-all | bytes 540672 | tf_op jit(solution)/shard_map/all_to_all | solution.py:32
  59.5 0.2 reduce_sum.80
  59.7 0.1 broadcast_in_dim.47
  59.9 10.9 %all_to_all.34 = f32[16,1,4224]{2,1,0:T(1,128)S(1)} all-to-all(f32[16,1,4224]{2,1,0:T(1,128)S(1)} %broadcast_in_dim.47), channel_id=1, replica_groups={{0,64,128,192,256,320,384,448,8,72,136,200,264,328,392,456},{2,66,130,1..., dimensions={0} | all-to-all | bytes 540672 | tf_op jit(solution)/shard_map/all_to_all | solution.py:32
  70.7 0.2 reduce_sum.81
  70.9 5.0 %all_gather.26.packed_ref = f32[2,33,128]{2,1,0:T(8,128)S(1)} all-gather(f32[1,33,128]{2,1,0:T(8,128)S(1)} %bitcast.57), channel_id=1, replica_groups={{0,1},{2,3},{4,5},{6,7},{8,9},{10,11},{12,13},{14,15},{16,17},{18,19},{..., dimensions={0}, use_global_device_ids=true | all-gather | bytes 50688 | tf_op jit(solution)/shard_map/all_gather | solution.py:46
  75.9 5.2 %factor.5 = (f32[128,128]{1,0:T(8,128)S(1)}, f32[128,128]{1,0:T(8,128)S(1)}, f32[1,1]{1,0:T(1,128)}) custom-call(f32[2,33,128]{2,1,0:T(8,128)S(1)} %all_gather.26.packed_ref), custom_call_target="tpu_custom_call" | custom-call | tf_op jit(solution)/shard_map/factor/pallas_call | solution.py:164
  81.1 0.8 while.14
  81.9 0.0 copy-start
  81.9 1.2 %apply.5 = f32[1024,128]{1,0:T(8,128)} custom-call(f32[1024,128]{1,0:T(8,128)S(1)} %get-tuple-element.156, f32[128,128]{1,0:T(8,128)S(1)} %get-tuple-element.63.inverse_ref), custom_call_target="tpu_custom_call" | custom-call | tf_op jit(solution)/shard_map/apply/pallas_call | solution.py:203
  83.2 0.0 copy-done
  (7 shorter events, 0.1 us)
Async XLA Ops:
  0.6 34.3 %all-to-all-start.2 = ((f32[512,2,128]{2,1,0:T(2,128)}), f32[512,2,128]{2,1,0:T(2,128)S(1)}, u32[]{:S(2)}, u32[]{:S(2)}) async-start(f32[512,2,128]{2,1,0:T(2,128)} %bitcast.56), calls=%async_computation.2 | async-start | bytes 1048576 | tf_op jit(solution)/shard_map/all_to_all | solution.py:32
  81.9 1.2 %copy-start = (f32[128,128]{1,0:T(8,128)}, f32[128,128]{1,0:T(8,128)S(1)}, u32[]{:S(2)}) copy-start(f32[128,128]{1,0:T(8,128)S(1)} %get-tuple-element.59) | copy-start | bytes 196612

commit v9 on v7

--- a/solution.py
+++ b/solution.py
@@ -16,6 +16,7 @@
 LIMIT = 4096.0
 CAP = 1e9
 GAIN = 64.0
+VMEM_LIMIT = 8 * 1024 * 1024
 
 
 def product(left, right, dims=((1,), (0,))):
@@ -170,6 +171,7 @@
         in_specs=[whole],
         out_specs=[whole] * 3,
         scratch_shapes=[pltpu.VMEM((order, 2 * order), jnp.float32)],
+        compiler_params=pltpu.CompilerParams(vmem_limit_bytes=VMEM_LIMIT),
         name="factor",
     )(packed)
     return inverse, upper, spread.reshape(())
@@ -211,6 +213,7 @@
             pltpu.VMEM((blocks * LANES, order), jnp.float32),
             pltpu.SemaphoreType.DMA((blocks,)),
         ],
+        compiler_params=pltpu.CompilerParams(vmem_limit_bytes=VMEM_LIMIT),
         name="apply",
     )(tiles, inverse)
 

time: 81.8 us -> 80.8 us (0.988)
  Pallas kernels: 7.26 us -> 6.42 us
    pallas_call x1, Pallas kernels: 6.04 us -> 5.19 us  [factor(): pl.pallas_call(functools.partial(factor_kernel, root), out_shape=[shape,...]
where the time goes in v9:
time: 80.8 us; the launch traced here: 80.5 us
  blocking collectives  36.6 us (45%)
  starting transfers between devices  17.1 us (21%)
  waiting for transfers between devices  17.1 us (21%)
  Pallas kernels  6.42 us (8%)
  between operations  0.91 us (1%)
  loops' own time  0.83 us (1%)
    all_to_all x2, blocking collectives, exchange(): lax.all_to_all(pieces, axis, split_axis=0, concat_axis=0, axis_index_grou...  28.9 us
    all_to_all x1, starting transfers between devices, exchange(): lax.all_to_all(pieces, axis, split_axis=0, concat_axis=0, axis_index_grou...  17.1 us
    all_to_all x1, waiting for transfers between devices, exchange(): lax.all_to_all(pieces, axis, split_axis=0, concat_axis=0, axis_index_grou...  17.1 us
    all_gather x2, blocking collectives, paired(): return lax.all_gather(part, EVERY, axis_index_groups=groups)  7.67 us
    pallas_call x1, Pallas kernels, factor(): pl.pallas_call(functools.partial(factor_kernel, root), out_shape=[shape,...  5.19 us
  transfers between devices with their start and end apart: 1, of which 1 were waited for; matrix products, arithmetic and copies ran while one was open for 0% of the time, Pallas kernels for 0%

profile of v9, /device:TPU:1, one launch (start us, length us, event | category | flops | bytes accessed | tf_op | source)
XLA Modules:
  0.0 80.5 jit_solution(12113363166458674801)
XLA Ops:
  0.6 17.1 %all-to-all-start.2 = ((f32[512,2,128]{2,1,0:T(2,128)}), f32[512,2,128]{2,1,0:T(2,128)S(1)}, u32[]{:S(2)}, u32[]{:S(2)}) async-start(f32[512,2,128]{2,1,0:T(2,128)} %bitcast.56), calls=%async_computation.2 | async-start | bytes 1048576 | tf_op jit(solution)/shard_map/all_to_all | solution.py:33
  17.8 17.1 %all-to-all-done.2 = f32[512,2,128]{2,1,0:T(2,128)S(1)} async-done(((f32[512,2,128]{2,1,0:T(2,128)}), f32[512,2,128]{2,1,0:T(2,128)S(1)}, u32[]{:S(2)}, u32[]{:S(2)}) %all-to-all-start.2) | async-done | bytes 524320 | tf_op jit(solution)/shard_map/all_to_all | solution.py:33
  35.0 0.6 fusion.1
  35.7 0.1 fusion.6
  35.8 0.1 slice_select_fusion.3
  35.9 5.0 %all-gather.3 = f32[2,66,128]{2,1,0:T(8,128)S(1)} all-gather(f32[1,66,128]{2,1,0:T(8,128)S(1)} %maximum_bitcast_fusion.1), channel_id=3, replica_groups={{0,1},{2,3},{4,5},{6,7},{8,9},{10,11},{12,13},{14,15},{16,17},{18,19},{..., dimensions={0}, use_global_device_ids=true | all-gather | bytes 101376 | tf_op jit(solution)/shard_map/all_gather | solution.py:47
  40.9 0.1 broadcast_in_dim.46
  41.1 16.1 %all_to_all.33 = f32[16,1,4224]{2,1,0:T(1,128)S(1)} all-to-all(f32[16,1,4224]{2,1,0:T(1,128)S(1)} %broadcast_in_dim.46), channel_id=1, replica_groups={{0,16,32,48,2,18,34,50,4,20,36,52,6,22,38,54},{8,24,40,56,10,26,42,58,1..., dimensions={0} | all-to-all | bytes 540672 | tf_op jit(solution)/shard_map/all_to_all | solution.py:33
  57.2 0.2 reduce_sum.80
  57.3 0.1 broadcast_in_dim.47
  57.5 12.8 %all_to_all.34 = f32[16,1,4224]{2,1,0:T(1,128)S(1)} all-to-all(f32[16,1,4224]{2,1,0:T(1,128)S(1)} %broadcast_in_dim.47), channel_id=1, replica_groups={{0,64,128,192,256,320,384,448,8,72,136,200,264,328,392,456},{2,66,130,1..., dimensions={0} | all-to-all | bytes 540672 | tf_op jit(solution)/shard_map/all_to_all | solution.py:33
  70.3 0.2 reduce_sum.81
  70.4 2.7 %all_gather.26.packed_ref = f32[2,33,128]{2,1,0:T(8,128)S(1)} all-gather(f32[1,33,128]{2,1,0:T(8,128)S(1)} %bitcast.57), channel_id=1, replica_groups={{0,1},{2,3},{4,5},{6,7},{8,9},{10,11},{12,13},{14,15},{16,17},{18,19},{..., dimensions={0}, use_global_device_ids=true | all-gather | bytes 50688 | tf_op jit(solution)/shard_map/all_gather | solution.py:47
  73.1 5.2 %factor.5 = (f32[128,128]{1,0:T(8,128)S(1)}, f32[128,128]{1,0:T(8,128)S(1)}, f32[1,1]{1,0:T(1,128)}) custom-call(f32[2,33,128]{2,1,0:T(8,128)S(1)} %all_gather.26.packed_ref), custom_call_target="tpu_custom_call" | custom-call | tf_op jit(solution)/shard_map/factor/pallas_call | solution.py:168
  78.3 0.8 %while.14 = (f32[128,128]{1,0:T(8,128)S(1)}, f32[128,128]{1,0:T(8,128)S(1)}, f32[]{:T(128)}, f32[1024,128]{1,0:T(8,128)S(1)}, f32[]{:T(128)}, /*index=5*/u32[]{:...) while((f32[128,128]{1,0:T(8,128)S(1)}, f32[128,128]{1,0:T(8,128)S(1)}, ...), condition=%wide.region_9.10_spmd, body=%wide.region_4.9_spmd.sunk | while | flops 251850944 | bytes 4300128 | solution.py:243
  79.1 0.0 copy-start
  79.1 1.2 %apply.5 = f32[1024,128]{1,0:T(8,128)} custom-call(f32[1024,128]{1,0:T(8,128)S(1)} %get-tuple-element.156, f32[128,128]{1,0:T(8,128)S(1)} %get-tuple-element.63.inverse_ref), custom_call_target="tpu_custom_call" | custom-call | tf_op jit(solution)/shard_map/apply/pallas_call | solution.py:207
  80.4 0.0 copy-done
  (7 shorter events, 0.1 us)
Async XLA Ops:
  0.6 34.3 %all-to-all-start.2 = ((f32[512,2,128]{2,1,0:T(2,128)}), f32[512,2,128]{2,1,0:T(2,128)S(1)}, u32[]{:S(2)}, u32[]{:S(2)}) async-start(f32[512,2,128]{2,1,0:T(2,128)} %bitcast.56), calls=%async_computation.2 | async-start | bytes 1048576 | tf_op jit(solution)/shard_map/all_to_all | solution.py:33
  79.1 1.2 %copy-start = (f32[128,128]{1,0:T(8,128)}, f32[128,128]{1,0:T(8,128)S(1)}, u32[]{:S(2)}) copy-start(f32[128,128]{1,0:T(8,128)S(1)} %get-tuple-element.59) | copy-start | bytes 196612

commit v10 on v9

--- a/solution.py
+++ b/solution.py
@@ -53,10 +53,10 @@
     places = np.arange(wide * narrow).reshape(side // 2, 2, side // 2, 2, narrow // 2, 2)
     pairs = places.reshape(-1, 2).tolist()
     even, odd = places[..., 0], places[..., 1]
-    first = [even.transpose(0, 1, 3, 4, 2), odd.transpose(1, 2, 3, 4, 0)]
-    second = [even.transpose(2, 4, 3, 0, 1), odd.transpose(0, 4, 1, 2, 3)]
-    first = np.concatenate([part.reshape(-1, narrow // 2 * (side // 2)) for part in first])
-    second = np.concatenate([part.reshape(-1, 2 * side) for part in second])
+    first = [even.transpose(2, 4, 3, 0, 1), odd.transpose(0, 4, 1, 2, 3)]
+    second = [even.transpose(0, 1, 3, 4, 2), odd.transpose(1, 2, 3, 4, 0)]
+    first = np.concatenate([part.reshape(-1, 2 * side) for part in first])
+    second = np.concatenate([part.reshape(-1, narrow // 2 * (side // 2)) for part in second])
     half = packed.shape[0] // 2
     both = jnp.sum(paired(packed, pairs), axis=0)
     part = lax.dynamic_slice_in_dim(both, lax.axis_index("narrow") % 2 * half, half, axis=0)

time: 80.8 us -> 82.5 us (1.021)
  blocking collectives: 36.6 us -> 38.3 us
    all_gather x2, blocking collectives: 7.67 us -> 9.61 us  [paired(): return lax.all_gather(part, EVERY, axis_index_groups=groups)]
where the time goes in v10:
time: 82.5 us; the launch traced here: 82.3 us
  blocking collectives  38.3 us (46%)
  starting transfers between devices  17.1 us (21%)
  waiting for transfers between devices  17.1 us (21%)
  Pallas kernels  6.42 us (8%)
  between operations  0.91 us (1%)
  loops' own time  0.83 us (1%)
    all_to_all x2, blocking collectives, exchange(): lax.all_to_all(pieces, axis, split_axis=0, concat_axis=0, axis_index_grou...  28.7 us
    all_to_all x1, starting transfers between devices, exchange(): lax.all_to_all(pieces, axis, split_axis=0, concat_axis=0, axis_index_grou...  17.1 us
    all_to_all x1, waiting for transfers between devices, exchange(): lax.all_to_all(pieces, axis, split_axis=0, concat_axis=0, axis_index_grou...  17.1 us
    all_gather x2, blocking collectives, paired(): return lax.all_gather(part, EVERY, axis_index_groups=groups)  9.61 us
    pallas_call x1, Pallas kernels, factor(): pl.pallas_call(functools.partial(factor_kernel, root), out_shape=[shape,...  5.19 us
  transfers between devices with their start and end apart: 1, of which 1 were waited for; matrix products, arithmetic and copies ran while one was open for 0% of the time, Pallas kernels for 0%

profile of v10, /device:TPU:1, one launch (start us, length us, event | category | flops | bytes accessed | tf_op | source)
XLA Modules:
  0.0 82.3 jit_solution(14032815538174007855)
XLA Ops:
  0.6 17.1 %all-to-all-start.2 = ((f32[512,2,128]{2,1,0:T(2,128)}), f32[512,2,128]{2,1,0:T(2,128)S(1)}, u32[]{:S(2)}, u32[]{:S(2)}) async-start(f32[512,2,128]{2,1,0:T(2,128)} %bitcast.56), calls=%async_computation.2 | async-start | bytes 1048576 | tf_op jit(solution)/shard_map/all_to_all | solution.py:33
  17.8 17.1 %all-to-all-done.2 = f32[512,2,128]{2,1,0:T(2,128)S(1)} async-done(((f32[512,2,128]{2,1,0:T(2,128)}), f32[512,2,128]{2,1,0:T(2,128)S(1)}, u32[]{:S(2)}, u32[]{:S(2)}) %all-to-all-start.2) | async-done | bytes 524320 | tf_op jit(solution)/shard_map/all_to_all | solution.py:33
  35.0 0.6 fusion.1
  35.7 0.1 fusion.6
  35.8 0.1 slice_select_fusion.3
  35.9 5.0 %all-gather.3 = f32[2,66,128]{2,1,0:T(8,128)S(1)} all-gather(f32[1,66,128]{2,1,0:T(8,128)S(1)} %maximum_bitcast_fusion.1), channel_id=3, replica_groups={{0,1},{2,3},{4,5},{6,7},{8,9},{10,11},{12,13},{14,15},{16,17},{18,19},{..., dimensions={0}, use_global_device_ids=true | all-gather | bytes 101376 | tf_op jit(solution)/shard_map/all_gather | solution.py:47
  40.9 0.1 broadcast_in_dim.46
  41.1 12.1 %all_to_all.33 = f32[16,1,4224]{2,1,0:T(1,128)S(1)} all-to-all(f32[16,1,4224]{2,1,0:T(1,128)S(1)} %broadcast_in_dim.46), channel_id=1, replica_groups={{0,64,128,192,256,320,384,448,8,72,136,200,264,328,392,456},{2,66,130,1..., dimensions={0} | all-to-all | bytes 540672 | tf_op jit(solution)/shard_map/all_to_all | solution.py:33
  53.1 0.2 reduce_sum.80
  53.3 0.1 broadcast_in_dim.47
  53.4 16.6 %all_to_all.34 = f32[16,1,4224]{2,1,0:T(1,128)S(1)} all-to-all(f32[16,1,4224]{2,1,0:T(1,128)S(1)} %broadcast_in_dim.47), channel_id=1, replica_groups={{0,16,32,48,2,18,34,50,4,20,36,52,6,22,38,54},{8,24,40,56,10,26,42,58,1..., dimensions={0} | all-to-all | bytes 540672 | tf_op jit(solution)/shard_map/all_to_all | solution.py:33
  70.0 0.2 reduce_sum.81
  70.2 4.6 %all_gather.26.packed_ref = f32[2,33,128]{2,1,0:T(8,128)S(1)} all-gather(f32[1,33,128]{2,1,0:T(8,128)S(1)} %bitcast.57), channel_id=1, replica_groups={{0,1},{2,3},{4,5},{6,7},{8,9},{10,11},{12,13},{14,15},{16,17},{18,19},{..., dimensions={0}, use_global_device_ids=true | all-gather | bytes 50688 | tf_op jit(solution)/shard_map/all_gather | solution.py:47
  74.8 5.2 %factor.5 = (f32[128,128]{1,0:T(8,128)S(1)}, f32[128,128]{1,0:T(8,128)S(1)}, f32[1,1]{1,0:T(1,128)}) custom-call(f32[2,33,128]{2,1,0:T(8,128)S(1)} %all_gather.26.packed_ref), custom_call_target="tpu_custom_call" | custom-call | tf_op jit(solution)/shard_map/factor/pallas_call | solution.py:168
  80.0 0.8 %while.14 = (f32[128,128]{1,0:T(8,128)S(1)}, f32[128,128]{1,0:T(8,128)S(1)}, f32[]{:T(128)}, f32[1024,128]{1,0:T(8,128)S(1)}, f32[]{:T(128)}, /*index=5*/u32[]{:...) while((f32[128,128]{1,0:T(8,128)S(1)}, f32[128,128]{1,0:T(8,128)S(1)}, ...), condition=%wide.region_9.10_spmd, body=%wide.region_4.9_spmd.sunk | while | flops 251850944 | bytes 4300128 | solution.py:243
  80.8 0.0 copy-start
  80.9 1.2 %apply.5 = f32[1024,128]{1,0:T(8,128)} custom-call(f32[1024,128]{1,0:T(8,128)S(1)} %get-tuple-element.156, f32[128,128]{1,0:T(8,128)S(1)} %get-tuple-element.63.inverse_ref), custom_call_target="tpu_custom_call" | custom-call | tf_op jit(solution)/shard_map/apply/pallas_call | solution.py:207
  82.1 0.0 copy-done
  (7 shorter events, 0.1 us)
Async XLA Ops:
  0.6 34.3 %all-to-all-start.2 = ((f32[512,2,128]{2,1,0:T(2,128)}), f32[512,2,128]{2,1,0:T(2,128)S(1)}, u32[]{:S(2)}, u32[]{:S(2)}) async-start(f32[512,2,128]{2,1,0:T(2,128)} %bitcast.56), calls=%async_computation.2 | async-start | bytes 1048576 | tf_op jit(solution)/shard_map/all_to_all | solution.py:33
  80.8 1.2 %copy-start = (f32[128,128]{1,0:T(8,128)}, f32[128,128]{1,0:T(8,128)S(1)}, u32[]{:S(2)}) copy-start(f32[128,128]{1,0:T(8,128)S(1)} %get-tuple-element.59) | copy-start | bytes 196612

commit v11 on v9

--- a/solution.py
+++ b/solution.py
@@ -146,15 +146,14 @@
         work[base:end, :] = rows
         if end < order:
             high, middle, low = split(rows)
-            first = jnp.concatenate([high, high, middle, high, low, middle], axis=0)
-            second = jnp.concatenate([high, middle, high, low, high, middle], axis=0)
-            update = lax.dot_general(
-                first[:, :order],
-                second,
-                (((0,), (0,)), ((), ())),
-                preferred_element_type=jnp.float32,
-            )
-            work[end:, :] -= update[end:, :]
+            none = jnp.zeros_like(high)
+            turned = jnp.concatenate([high, middle, low, high], axis=0)[:, :order]
+            turned = jnp.transpose(turned)[end:, :]
+            most = jnp.concatenate([high, high, high, none], axis=0)
+            rest = jnp.concatenate([middle, middle, none, low], axis=0)
+            for side in (slice(0, order), slice(order, 2 * order)):
+                both = bf16_product(turned, jnp.concatenate([most[:, side], rest[:, side]], axis=1))
+                work[end:, side] -= both[:, :order] + both[:, order:]
     inverse = jnp.where(across <= down, work[:, order:], 0.0)
     spread_ref[...] = jnp.minimum(jnp.sum(inverse * inverse, keepdims=True), CAP)
     inverse_ref[...] = inverse * (scale * root)

time: 80.8 us -> 80.7 us (level)
  no operation moved by 1% of the time
where the time goes in v11:
time: 80.7 us; the launch traced here: 80.4 us
  blocking collectives  36.6 us (45%)
  starting transfers between devices  17.1 us (21%)
  waiting for transfers between devices  17.1 us (21%)
  Pallas kernels  6.24 us (8%)
  between operations  0.91 us (1%)
  loops' own time  0.83 us (1%)
    all_to_all x2, blocking collectives, exchange(): lax.all_to_all(pieces, axis, split_axis=0, concat_axis=0, axis_index_grou...  28.9 us
    all_to_all x1, starting transfers between devices, exchange(): lax.all_to_all(pieces, axis, split_axis=0, concat_axis=0, axis_index_grou...  17.1 us
    all_to_all x1, waiting for transfers between devices, exchange(): lax.all_to_all(pieces, axis, split_axis=0, concat_axis=0, axis_index_grou...  17.1 us
    all_gather x2, blocking collectives, paired(): return lax.all_gather(part, EVERY, axis_index_groups=groups)  7.67 us
    pallas_call x1, Pallas kernels, factor(): pl.pallas_call(functools.partial(factor_kernel, root), out_shape=[shape,...  5.02 us
  transfers between devices with their start and end apart: 1, of which 1 were waited for; matrix products, arithmetic and copies ran while one was open for 0% of the time, Pallas kernels for 0%

profile of v11, /device:TPU:1, one launch (start us, length us, event | category | flops | bytes accessed | tf_op | source)
XLA Modules:
  0.0 80.4 jit_solution(6256668038278689072)
XLA Ops:
  0.6 17.1 %all-to-all-start.2 = ((f32[512,2,128]{2,1,0:T(2,128)}), f32[512,2,128]{2,1,0:T(2,128)S(1)}, u32[]{:S(2)}, u32[]{:S(2)}) async-start(f32[512,2,128]{2,1,0:T(2,128)} %bitcast.56), calls=%async_computation.2 | async-start | bytes 1048576 | tf_op jit(solution)/shard_map/all_to_all | solution.py:33
  17.8 17.1 %all-to-all-done.2 = f32[512,2,128]{2,1,0:T(2,128)S(1)} async-done(((f32[512,2,128]{2,1,0:T(2,128)}), f32[512,2,128]{2,1,0:T(2,128)S(1)}, u32[]{:S(2)}, u32[]{:S(2)}) %all-to-all-start.2) | async-done | bytes 524320 | tf_op jit(solution)/shard_map/all_to_all | solution.py:33
  35.0 0.6 fusion.1
  35.7 0.1 fusion.6
  35.8 0.1 slice_select_fusion.3
  35.9 5.0 %all-gather.3 = f32[2,66,128]{2,1,0:T(8,128)S(1)} all-gather(f32[1,66,128]{2,1,0:T(8,128)S(1)} %maximum_bitcast_fusion.1), channel_id=3, replica_groups={{0,1},{2,3},{4,5},{6,7},{8,9},{10,11},{12,13},{14,15},{16,17},{18,19},{..., dimensions={0}, use_global_device_ids=true | all-gather | bytes 101376 | tf_op jit(solution)/shard_map/all_gather | solution.py:47
  40.9 0.1 broadcast_in_dim.46
  41.1 16.1 %all_to_all.33 = f32[16,1,4224]{2,1,0:T(1,128)S(1)} all-to-all(f32[16,1,4224]{2,1,0:T(1,128)S(1)} %broadcast_in_dim.46), channel_id=1, replica_groups={{0,16,32,48,2,18,34,50,4,20,36,52,6,22,38,54},{8,24,40,56,10,26,42,58,1..., dimensions={0} | all-to-all | bytes 540672 | tf_op jit(solution)/shard_map/all_to_all | solution.py:33
  57.2 0.2 reduce_sum.80
  57.3 0.1 broadcast_in_dim.47
  57.5 12.8 %all_to_all.34 = f32[16,1,4224]{2,1,0:T(1,128)S(1)} all-to-all(f32[16,1,4224]{2,1,0:T(1,128)S(1)} %broadcast_in_dim.47), channel_id=1, replica_groups={{0,64,128,192,256,320,384,448,8,72,136,200,264,328,392,456},{2,66,130,1..., dimensions={0} | all-to-all | bytes 540672 | tf_op jit(solution)/shard_map/all_to_all | solution.py:33
  70.3 0.2 reduce_sum.81
  70.4 2.7 %all_gather.26.packed_ref = f32[2,33,128]{2,1,0:T(8,128)S(1)} all-gather(f32[1,33,128]{2,1,0:T(8,128)S(1)} %bitcast.57), channel_id=1, replica_groups={{0,1},{2,3},{4,5},{6,7},{8,9},{10,11},{12,13},{14,15},{16,17},{18,19},{..., dimensions={0}, use_global_device_ids=true | all-gather | bytes 50688 | tf_op jit(solution)/shard_map/all_gather | solution.py:47
  73.1 5.0 %factor.5 = (f32[128,128]{1,0:T(8,128)S(1)}, f32[128,128]{1,0:T(8,128)S(1)}, f32[1,1]{1,0:T(1,128)}) custom-call(f32[2,33,128]{2,1,0:T(8,128)S(1)} %all_gather.26.packed_ref), custom_call_target="tpu_custom_call" | custom-call | tf_op jit(solution)/shard_map/factor/pallas_call | solution.py:167
  78.1 0.8 %while.14 = (f32[128,128]{1,0:T(8,128)S(1)}, f32[128,128]{1,0:T(8,128)S(1)}, f32[]{:T(128)}, f32[1024,128]{1,0:T(8,128)S(1)}, f32[]{:T(128)}, /*index=5*/u32[]{:...) while((f32[128,128]{1,0:T(8,128)S(1)}, f32[128,128]{1,0:T(8,128)S(1)}, ...), condition=%wide.region_9.10_spmd, body=%wide.region_4.9_spmd.sunk | while | flops 251850944 | bytes 4300128 | solution.py:242
  79.0 0.0 copy-start
  79.0 1.2 %apply.5 = f32[1024,128]{1,0:T(8,128)} custom-call(f32[1024,128]{1,0:T(8,128)S(1)} %get-tuple-element.156, f32[128,128]{1,0:T(8,128)S(1)} %get-tuple-element.63.inverse_ref), custom_call_target="tpu_custom_call" | custom-call | tf_op jit(solution)/shard_map/apply/pallas_call | solution.py:206
  80.2 0.0 copy-done
  (7 shorter events, 0.1 us)
Async XLA Ops:
  0.6 34.3 %all-to-all-start.2 = ((f32[512,2,128]{2,1,0:T(2,128)}), f32[512,2,128]{2,1,0:T(2,128)S(1)}, u32[]{:S(2)}, u32[]{:S(2)}) async-start(f32[512,2,128]{2,1,0:T(2,128)} %bitcast.56), calls=%async_computation.2 | async-start | bytes 1048576 | tf_op jit(solution)/shard_map/all_to_all | solution.py:33
  79.0 1.2 %copy-start = (f32[128,128]{1,0:T(8,128)}, f32[128,128]{1,0:T(8,128)S(1)}, u32[]{:S(2)}) copy-start(f32[128,128]{1,0:T(8,128)S(1)} %get-tuple-element.59) | copy-start | bytes 196612
